TPU v7x, 256 devices: a whole 4x4x8 slice. The times are simulated.
256 devices in a mesh: section: 8 (over z), dp: 32 (over x, y, core).
Axes of the slice: x: 4, y: 4, z: 8, core: 2. Of those that a mesh axis runs over, the one named last changes fastest.
Arguments:
- x0: bfloat16 [4, 1024, 5120], P(None, 'dp'), may hold values from -6 to 6
- w_key: bfloat16 [8, 5120, 512], P('section'), may hold values from -0.078125 to 0.078125
- w_value: bfloat16 [8, 5120, 512], P('section'), may hold values from -0.078125 to 0.078125
- w_score: float32 [5120], replicated, may hold values from -0.078125 to 0.078125
- segments: int32 [4, 1024], P(None, 'dp'), may hold values from 0 to 31, as said below
- lengths: int32 [4, 32], P(None, 'dp'), may hold values from 1 to 32, as said below
- grades: int32 [4, 1024], P(None, 'dp'), may hold values from 0 to 3
Outputs:
- grad_key: float32 [8, 5120, 512], P('section', 'dp')
- grad_value: float32 [8, 5120, 512], P('section', 'dp')
Inputs may be any that keep to these rules, and one draw needn't show every extreme that they name: `segments`: within each packed row of 32 slots the ids start at 0 and never fall; in every draw some packed row has a new id at every slot. `lengths`: every packed row has its live tokens at the front; in every draw some packed row is full.
All inputs are finite; a program needn't handle non-finite values.
Results may differ from a plain program's by a relative error of at most 0.035.
Values may be sent and summed in bfloat16 or wider, within the bound.
A program may use at most 128 MiB of HBM per device.

v0:
```python
import jax
import jax.numpy as jnp
from jax import lax
from jax.sharding import PartitionSpec as P

HD = 128
KV_HEADS = 4


EPS = 1e-06
THETA = 1000000.0


def shifted(value, axis, steps):
    count = lax.axis_size(axis)
    first, last = (max(0, -steps), min(count, count - steps))
    return lax.ppermute(value, axis, [(source, source + steps) for source in range(first, last)])


def rope_tables(segments):
    width = segments.shape[-1]
    index = jnp.arange(width, dtype=jnp.int32)
    section_begin_offsets = jnp.concatenate(
        [jnp.ones(segments.shape[:-1] + (1,), bool), segments[..., 1:] != segments[..., :-1]],
        axis=-1,
    )
    leading_half = lax.cummax(
        jnp.where(section_begin_offsets, index, jnp.int32(0)), axis=segments.ndim - 1
    )
    offset = (index - leading_half).astype(jnp.float32)
    freqs = THETA ** (-(jnp.arange(HD // 2, dtype=jnp.float32) * 2.0) / HD)
    angles = offset[..., None] * freqs
    return (jnp.cos(angles), jnp.sin(angles))


def allowed_mask(segments, lengths):
    width = segments.shape[-1]
    index = jnp.arange(width, dtype=jnp.int32)
    same = segments[..., :, None] == segments[..., None, :]
    causal = index[None, :] <= index[:, None]
    live = index < lengths
    allowed = same & causal & live[..., :, None] & live[..., None, :]
    return allowed | jnp.eye(width, dtype=bool)


def rotate(vectors, cosine, sine_table):
    half = HD // 2
    cosine_value = cosine[..., :, None, :]
    sine_value = sine_table[..., :, None, :]
    leading_half, trailing_half = (vectors[..., :half], vectors[..., half:])
    return jnp.concatenate(
        [
            leading_half * cosine_value - trailing_half * sine_value,
            trailing_half * cosine_value + leading_half * sine_value,
        ],
        axis=-1,
    )


def rotate_back(grads, cosine, sine_table):
    half = HD // 2
    cosine_value = cosine[..., :, None, :]
    sine_value = sine_table[..., :, None, :]
    leading_half, trailing_half = (grads[..., :half], grads[..., half:])
    return jnp.concatenate(
        [
            leading_half * cosine_value + trailing_half * sine_value,
            trailing_half * cosine_value - leading_half * sine_value,
        ],
        axis=-1,
    )


def normalize(hidden):
    hfull = hidden.astype(jnp.float32)
    scale = lax.rsqrt(jnp.mean(hfull * hfull, axis=-1, keepdims=True) + EPS)
    return (hfull, scale)


def heads(array):
    return array.reshape(array.shape[:-1] + (KV_HEADS, HD))


def times_transposed(left, right):
    return lax.dot_general(
        left, right, (((1,), (1,)), ((), ())), preferred_element_type=jnp.float32
    )


def over_tokens(left, right):
    return lax.dot_general(
        left, right, (((0,), (0,)), ((), ())), preferred_element_type=jnp.float32
    )


def attend(keys_b, values_b, allowed):
    scores = jnp.einsum("ihd,jhd->hij", keys_b, keys_b, preferred_element_type=jnp.float32) / HD
    scores = jnp.where(allowed[None, :, :], scores, -1e30)
    probs = jax.nn.softmax(scores, axis=-1)
    probs_b = probs.astype(jnp.bfloat16)
    mixed = jnp.einsum("hij,jhd->ihd", probs_b, values_b, preferred_element_type=jnp.float32)
    return (probs, probs_b, mixed)


def layer_forward(hidden, w_key, w_value, cosine, sine_table, allowed):
    hfull, scale = normalize(hidden)
    normed = (hfull * scale).astype(jnp.bfloat16)
    keys = jnp.dot(normed, w_key, preferred_element_type=jnp.float32)
    keys_b = rotate(heads(keys), cosine, sine_table).astype(jnp.bfloat16)
    values_b = heads(
        jnp.dot(normed, w_value, preferred_element_type=jnp.float32).astype(jnp.bfloat16)
    )
    probs, probs_b, mixed = attend(keys_b, values_b, allowed)
    mixed_b = mixed.astype(jnp.bfloat16).reshape(hidden.shape[0], KV_HEADS * HD)
    output = hfull + times_transposed(mixed_b, w_value)
    return (output.astype(jnp.bfloat16), keys_b, values_b)


def layer_backward(hidden, keys_b, values_b, grad_out, w_key, w_value, cosine, sine_table, allowed):
    width = hidden.shape[0]
    hfull, scale = normalize(hidden)
    probs, probs_b, mixed = attend(keys_b, values_b, allowed)
    mixed_b = mixed.astype(jnp.bfloat16).reshape(width, KV_HEADS * HD)
    grad_mixed = heads(
        jnp.dot(grad_out, w_value, preferred_element_type=jnp.float32).astype(jnp.bfloat16)
    )
    grad_probs = jnp.einsum(
        "ihd,jhd->hij", grad_mixed, values_b, preferred_element_type=jnp.float32
    )
    grad_values = jnp.einsum(
        "hij,ihd->jhd", probs_b, grad_mixed, preferred_element_type=jnp.float32
    )
    grad_values = grad_values.astype(jnp.bfloat16).reshape(width, KV_HEADS * HD)
    grad_scores = (
        probs * (grad_probs - jnp.sum(probs * grad_probs, axis=-1, keepdims=True))
    ).astype(jnp.bfloat16)
    grad_keys = jnp.einsum("hij,jhd->ihd", grad_scores, keys_b, preferred_element_type=jnp.float32)
    grad_keys = (
        grad_keys
        + jnp.einsum("hij,ihd->jhd", grad_scores, keys_b, preferred_element_type=jnp.float32)
    ) / HD
    grad_keys = (
        rotate_back(grad_keys, cosine, sine_table)
        .astype(jnp.bfloat16)
        .reshape(width, KV_HEADS * HD)
    )
    grad_normed = times_transposed(grad_keys, w_key) + times_transposed(grad_values, w_value)
    incoming_gradient = (
        grad_out.astype(jnp.float32)
        + scale * grad_normed
        - hfull * scale**3 * jnp.mean(grad_normed * hfull, axis=-1, keepdims=True)
    )
    return (incoming_gradient.astype(jnp.bfloat16), grad_keys, grad_values, mixed_b)


def loss_gradient(hidden, segments, length, grades, w_score):
    hfull, scale = normalize(hidden)
    xfull = hfull * scale
    score = jnp.dot(xfull, w_score, precision=lax.Precision.HIGHEST)
    width = segments.shape[-1]
    index = jnp.arange(width, dtype=jnp.int32)
    following = jnp.concatenate([segments[1:] != segments[:-1], jnp.ones((1,), bool)], axis=-1)
    ends = (index < length) & (following | (index == length - 1))
    target = jax.nn.softmax(jnp.where(ends, grades.astype(jnp.float32), -1e30), axis=-1)
    model = jax.nn.softmax(jnp.where(ends, score, -1e30), axis=-1)
    weight = jnp.where(ends, model - target, 0.0)
    grad_x = weight[:, None] * w_score
    grad_h = scale * grad_x - hfull * scale**3 * jnp.mean(grad_x * hfull, axis=-1, keepdims=True)
    return grad_h.astype(jnp.bfloat16)


def pick(array, slot):
    return lax.dynamic_index_in_dim(array, slot, 0, keepdims=False)


def place(array, slot, value, valid):
    kept = jnp.where(valid, value, pick(array, slot))
    return lax.dynamic_update_index_in_dim(array, kept, slot, 0)


def shards(x0, w_key, w_value, w_score, segments, lengths, grades):
    sections = lax.axis_size("section")
    section = lax.axis_index("section")
    micro, width, model_width = x0.shape
    key_proj = w_key[0]
    value_proj = w_value[0]
    features = key_proj.shape[1]
    cosine, sine_table = rope_tables(segments)
    allowed = allowed_mask(segments, lengths)
    ticks = micro + sections - 1
    row_zeros = jnp.zeros((width, model_width), jnp.bfloat16)

    def forward_tick(carry, tick):
        incoming, saved_in, saved_keys, saved_values, finals = carry
        offset = tick - section
        valid = (offset >= 0) & (offset < micro)
        slot = jnp.clip(offset, 0, micro - 1)
        current = jnp.where(section == 0, pick(x0, slot), incoming)
        produced, keys_b, values_b = layer_forward(
            current,
            key_proj,
            value_proj,
            pick(cosine, slot),
            pick(sine_table, slot),
            pick(allowed, slot),
        )
        saved_in = place(saved_in, slot, current, valid)
        saved_keys = place(saved_keys, slot, keys_b, valid)
        saved_values = place(saved_values, slot, values_b, valid)
        finals = place(finals, slot, produced, valid & (section == sections - 1))
        outgoing = shifted(produced, "section", 1)
        return ((outgoing, saved_in, saved_keys, saved_values, finals), None)

    act_store = jnp.zeros((micro, width, model_width), jnp.bfloat16)
    head_store = jnp.zeros((micro, width, KV_HEADS, HD), jnp.bfloat16)
    start = (row_zeros, act_store, head_store, head_store, act_store)
    carry, unused = lax.scan(forward_tick, start, jnp.arange(ticks, dtype=jnp.int32))
    saved_in, saved_keys, saved_values, finals = (carry[1], carry[2], carry[3], carry[4])

    def backward_tick(carry, tick):
        incoming, store_keys, store_values, store_out, store_mixed = carry
        offset = tick - (sections - 1 - section)
        valid = (offset >= 0) & (offset < micro)
        slot = jnp.clip(offset, 0, micro - 1)
        first_grad = loss_gradient(
            pick(finals, slot),
            pick(segments, slot),
            pick(lengths, slot),
            pick(grades, slot),
            w_score,
        )
        grad_out = jnp.where(section == sections - 1, first_grad, incoming)
        incoming_gradient, grad_keys, grad_values, mixed_b = layer_backward(
            pick(saved_in, slot),
            pick(saved_keys, slot),
            pick(saved_values, slot),
            grad_out,
            key_proj,
            value_proj,
            pick(cosine, slot),
            pick(sine_table, slot),
            pick(allowed, slot),
        )
        store_keys = place(store_keys, slot, grad_keys, valid)
        store_values = place(store_values, slot, grad_values, valid)
        store_out = place(store_out, slot, grad_out, valid)
        store_mixed = place(store_mixed, slot, mixed_b, valid)
        outgoing = shifted(incoming_gradient, "section", -1)
        return ((outgoing, store_keys, store_values, store_out, store_mixed), None)

    flat_store = jnp.zeros((micro, width, features), jnp.bfloat16)
    start = (row_zeros, flat_store, flat_store, act_store, flat_store)
    carry, unused = lax.scan(backward_tick, start, jnp.arange(ticks, dtype=jnp.int32))
    tokens = micro * width
    key_grads = carry[1].reshape(tokens, features)
    value_grads = carry[2].reshape(tokens, features)
    out_grads = carry[3].reshape(tokens, model_width)
    mixed_all = carry[4].reshape(tokens, features)
    hfull, scale = normalize(saved_in)
    normalized_everything = (hfull * scale).astype(jnp.bfloat16).reshape(tokens, model_width)
    part_key = over_tokens(normalized_everything, key_grads)
    part_value = over_tokens(normalized_everything, value_grads) + over_tokens(out_grads, mixed_all)
    summed = lax.psum_scatter(
        jnp.concatenate([part_key, part_value], axis=1).astype(jnp.bfloat16),
        "dp",
        scatter_dimension=0,
        tiled=True,
    ).astype(jnp.float32)
    grad_key = summed[:, :features]
    grad_value = summed[:, features:]
    return (grad_key[None], grad_value[None])


def solution(mesh):
    placed = (
        P(None, "dp", None),
        P("section", None, None),
        P("section", None, None),
        P(),
        P(None, "dp"),
        P(None, "dp"),
        P(None, "dp"),
    )
    return jax.shard_map(
        shards,
        mesh=mesh,
        in_specs=placed,
        out_specs=(P("section", "dp", None), P("section", "dp", None)),
        check_vma=False,
    )
```

profile of v0, /device:TPU:1, one launch (start us, length us, event | category | flops | bytes accessed | tf_op | source)
XLA Modules:
  0.0 938.3 jit_solution(5032071612566787471)
XLA Ops:
  13.2 344.8 %while.39 = (s32[]{:T(128)}, bf16[32,5120]{1,0:T(8,128)(2,1)}, bf16[4,32,5120]{2,1,0:T(8,128)(2,1)S(1)}, bf16[4,32,4,128]{3,1,2,0:T(8,128)(2,1)S(1)}, bf16[4,32,...) while((s32[]{:T(128)}, bf16[32,5120]{1,0:T(8,128)(2,1)}, ...), condition=%wide.region_5.6_spmd, body=%wide.region_1.5_spmd.sunk | while | flops 508158016 | bytes 24565244 | solution.py:217
  22.0 3.5 convolution_convert_fusion.7
  29.5 4.8 bitcast_dynamic-update-slice_fusion.7
  34.3 4.5 collective-permute-start
  40.3 5.2 collective-permute-done
  50.7 3.5 fusion.203
  55.0 3.5 convolution_convert_fusion.7
  62.5 4.8 bitcast_dynamic-update-slice_fusion.7
  67.3 4.1 collective-permute-start
  72.9 4.2 collective-permute-done
  86.7 3.5 convolution_convert_fusion.7
  94.2 4.8 bitcast_dynamic-update-slice_fusion.7
  99.0 4.1 collective-permute-start
  113.2 3.5 fusion.203
  117.4 3.5 convolution_convert_fusion.7
  124.9 4.8 bitcast_dynamic-update-slice_fusion.7
  129.8 4.1 collective-permute-start
  147.7 3.5 convolution_convert_fusion.7
  155.2 4.8 bitcast_dynamic-update-slice_fusion.7
  160.1 5.1 collective-permute-start
  179.0 3.5 convolution_convert_fusion.7
  186.5 4.8 bitcast_dynamic-update-slice_fusion.7
  191.4 5.3 collective-permute-start
  210.5 3.5 convolution_convert_fusion.7
  218.0 4.8 bitcast_dynamic-update-slice_fusion.7
  222.9 5.3 collective-permute-start
  242.0 3.5 convolution_convert_fusion.7
  249.5 4.8 bitcast_dynamic-update-slice_fusion.7
  254.3 5.0 collective-permute-start
  273.2 3.5 convolution_convert_fusion.7
  280.7 4.8 bitcast_dynamic-update-slice_fusion.7
  285.5 5.0 collective-permute-start
  304.4 3.5 convolution_convert_fusion.7
  311.9 4.8 bitcast_dynamic-update-slice_fusion.7
  316.7 5.0 collective-permute-start
  335.5 3.5 convolution_convert_fusion.7
  343.0 4.8 bitcast_dynamic-update-slice_fusion.7
  347.9 5.0 collective-permute-start
  362.7 407.1 %while.40 = (s32[]{:T(128)}, bf16[32,5120]{1,0:T(8,128)(2,1)S(1)}, bf16[4,32,512]{2,1,0:T(8,128)(2,1)}, bf16[4,32,512]{2,1,0:T(8,128)(2,1)}, bf16[4,32,5120]{2,1...) while((s32[]{:T(128)}, bf16[32,5120]{1,0:T(8,128)(2,1)S(1)}, ...), condition=%wide.region_19.20_spmd, body=%wide.region_7.19_spmd.sunk | while | flops 521950272 | bytes 48383308 | solution.py:253
  376.1 3.5 fusion.237
  382.1 4.3 fusion.240
  413.3 3.5 fusion.237
  419.3 4.3 fusion.240
  450.6 3.5 fusion.237
  456.5 4.3 fusion.240
  487.8 3.5 fusion.237
  493.7 4.3 fusion.240
  525.0 3.5 fusion.237
  531.0 4.3 fusion.240
  561.9 3.5 fusion.237
  567.9 4.3 fusion.240
  598.8 3.5 fusion.237
  604.7 4.3 fusion.240
  635.7 3.5 fusion.237
  641.6 4.3 fusion.240
  672.6 3.5 fusion.237
  678.5 4.3 fusion.240
  709.4 3.5 fusion.237
  715.4 4.3 fusion.240
  746.3 3.5 fusion.237
  752.3 4.3 fusion.240
  775.6 4.8 pad_maximum_fusion
  780.4 14.4 %copy.57 = bf16[5120,1024]{1,0:T(8,128)(2,1)} copy(bf16[5120,1024]{0,1:T(8,128)(2,1)} %pad_maximum_fusion) | data formatting | bytes 20971520
  794.8 133.5 %reduce-scatter.4.cloned.1.call-done = bf16[160,1024]{1,0:T(8,128)(2,1)} async-done(((bf16[5120,1024]{1,0:T(8,128)(2,1)}), bf16[160,1024]{1,0:T(8,128)(2,1)}) %reduce-scatter.4.cloned.1.call-update) | async-done | bytes 327696
  (809 shorter events, 507.2 us)
Async XLA Ops:
  7.2 921.2 %reduce-scatter.4.cloned.1.call-start = ((), (), s32[]{:S(2)}) async-start(), calls=%async_computation.1 | async-start | bytes 10813440
  34.3 11.1 %collective-permute-start = (bf16[32,5120]{1,0:T(8,128)(2,1)}, bf16[32,5120]{1,0:T(8,128)(2,1)S(1)}, u32[]{:S(2)}, u32[]{:S(2)}) collective-permute-start(bf16[32,5120]{1,0:T(8,128)(2,1)} %get-tuple-element.796), channel_id=1, source_target_pairs={{0,32},{32,64},{64,96},{96,128},{128,160},{160,192},{192,224},{1,3... | collective-permute-start | bytes 983048 | tf_op jit(solution)/shard_map/while/body/eval_jaxpr/ppermute | solution.py:17
  67.3 9.8 %collective-permute-start = (bf16[32,5120]{1,0:T(8,128)(2,1)}, bf16[32,5120]{1,0:T(8,128)(2,1)S(1)}, u32[]{:S(2)}, u32[]{:S(2)}) collective-permute-start(bf16[32,5120]{1,0:T(8,128)(2,1)} %get-tuple-element.796), channel_id=1, source_target_pairs={{0,32},{32,64},{64,96},{96,128},{128,160},{160,192},{192,224},{1,3... | collective-permute-start | bytes 983048 | tf_op jit(solution)/shard_map/while/body/eval_jaxpr/ppermute | solution.py:17
  99.0 8.9 collective-permute-start
  129.8 8.4 collective-permute-start
  160.1 9.4 %collective-permute-start = (bf16[32,5120]{1,0:T(8,128)(2,1)}, bf16[32,5120]{1,0:T(8,128)(2,1)S(1)}, u32[]{:S(2)}, u32[]{:S(2)}) collective-permute-start(bf16[32,5120]{1,0:T(8,128)(2,1)} %get-tuple-element.796), channel_id=1, source_target_pairs={{0,32},{32,64},{64,96},{96,128},{128,160},{160,192},{192,224},{1,3... | collective-permute-start | bytes 983048 | tf_op jit(solution)/shard_map/while/body/eval_jaxpr/ppermute | solution.py:17
  191.4 9.6 %collective-permute-start = (bf16[32,5120]{1,0:T(8,128)(2,1)}, bf16[32,5120]{1,0:T(8,128)(2,1)S(1)}, u32[]{:S(2)}, u32[]{:S(2)}) collective-permute-start(bf16[32,5120]{1,0:T(8,128)(2,1)} %get-tuple-element.796), channel_id=1, source_target_pairs={{0,32},{32,64},{64,96},{96,128},{128,160},{160,192},{192,224},{1,3... | collective-permute-start | bytes 983048 | tf_op jit(solution)/shard_map/while/body/eval_jaxpr/ppermute | solution.py:17
  222.9 9.6 %collective-permute-start = (bf16[32,5120]{1,0:T(8,128)(2,1)}, bf16[32,5120]{1,0:T(8,128)(2,1)S(1)}, u32[]{:S(2)}, u32[]{:S(2)}) collective-permute-start(bf16[32,5120]{1,0:T(8,128)(2,1)} %get-tuple-element.796), channel_id=1, source_target_pairs={{0,32},{32,64},{64,96},{96,128},{128,160},{160,192},{192,224},{1,3... | collective-permute-start | bytes 983048 | tf_op jit(solution)/shard_map/while/body/eval_jaxpr/ppermute | solution.py:17
  254.3 9.3 collective-permute-start
  285.5 9.3 collective-permute-start
  316.7 9.3 collective-permute-start
  347.9 9.3 collective-permute-start
  357.9 4.7 copy-start.3
  375.9 12.2 %copy-start.6 = (f32[32]{0:T(128)}, f32[32]{0:T(128)S(1)}, u32[]{:S(2)}) copy-start(f32[32]{0:T(128)S(1)} %broadcast_multiply_fusion.4) | copy-start | bytes 388 | tf_op jit(solution)/shard_map/while
  375.9 3.7 copy-start.7
  376.1 4.8 copy-start.9
  382.1 4.3 copy-start
  389.2 9.7 %collective-permute-start.1 = (bf16[32,5120]{1,0:T(8,128)(2,1)}, bf16[32,5120]{1,0:T(8,128)(2,1)}, u32[]{:S(2)}, u32[]{:S(2)}) collective-permute-start(bf16[32,5120]{1,0:T(8,128)(2,1)} %fusion.242), channel_id=1, source_target_pairs={{32,0},{64,32},{96,64},{128,96},{160,128},{192,160},{224,192},{33,... | collective-permute-start | bytes 983048 | tf_op jit(solution)/shard_map/while/body/eval_jaxpr/ppermute | solution.py:17
  413.1 12.2 %copy-start.6 = (f32[32]{0:T(128)}, f32[32]{0:T(128)S(1)}, u32[]{:S(2)}) copy-start(f32[32]{0:T(128)S(1)} %broadcast_multiply_fusion.4) | copy-start | bytes 388 | tf_op jit(solution)/shard_map/while
  413.1 3.7 copy-start.7
  413.3 4.8 copy-start.9
  419.3 4.3 copy-start
  426.5 9.7 %collective-permute-start.1 = (bf16[32,5120]{1,0:T(8,128)(2,1)}, bf16[32,5120]{1,0:T(8,128)(2,1)}, u32[]{:S(2)}, u32[]{:S(2)}) collective-permute-start(bf16[32,5120]{1,0:T(8,128)(2,1)} %fusion.242), channel_id=1, source_target_pairs={{32,0},{64,32},{96,64},{128,96},{160,128},{192,160},{224,192},{33,... | collective-permute-start | bytes 983048 | tf_op jit(solution)/shard_map/while/body/eval_jaxpr/ppermute | solution.py:17
  450.3 12.2 %copy-start.6 = (f32[32]{0:T(128)}, f32[32]{0:T(128)S(1)}, u32[]{:S(2)}) copy-start(f32[32]{0:T(128)S(1)} %broadcast_multiply_fusion.4) | copy-start | bytes 388 | tf_op jit(solution)/shard_map/while
  450.4 3.7 copy-start.7
  450.5 4.8 copy-start.9
  456.5 4.3 copy-start
  463.7 9.7 %collective-permute-start.1 = (bf16[32,5120]{1,0:T(8,128)(2,1)}, bf16[32,5120]{1,0:T(8,128)(2,1)}, u32[]{:S(2)}, u32[]{:S(2)}) collective-permute-start(bf16[32,5120]{1,0:T(8,128)(2,1)} %fusion.242), channel_id=1, source_target_pairs={{32,0},{64,32},{96,64},{128,96},{160,128},{192,160},{224,192},{33,... | collective-permute-start | bytes 983048 | tf_op jit(solution)/shard_map/while/body/eval_jaxpr/ppermute | solution.py:17
  487.6 12.2 %copy-start.6 = (f32[32]{0:T(128)}, f32[32]{0:T(128)S(1)}, u32[]{:S(2)}) copy-start(f32[32]{0:T(128)S(1)} %broadcast_multiply_fusion.4) | copy-start | bytes 388 | tf_op jit(solution)/shard_map/while
  487.6 3.7 copy-start.7
  487.8 4.8 copy-start.9
  493.7 4.3 copy-start
  500.9 9.7 %collective-permute-start.1 = (bf16[32,5120]{1,0:T(8,128)(2,1)}, bf16[32,5120]{1,0:T(8,128)(2,1)}, u32[]{:S(2)}, u32[]{:S(2)}) collective-permute-start(bf16[32,5120]{1,0:T(8,128)(2,1)} %fusion.242), channel_id=1, source_target_pairs={{32,0},{64,32},{96,64},{128,96},{160,128},{192,160},{224,192},{33,... | collective-permute-start | bytes 983048 | tf_op jit(solution)/shard_map/while/body/eval_jaxpr/ppermute | solution.py:17
  524.8 12.2 %copy-start.6 = (f32[32]{0:T(128)}, f32[32]{0:T(128)S(1)}, u32[]{:S(2)}) copy-start(f32[32]{0:T(128)S(1)} %broadcast_multiply_fusion.4) | copy-start | bytes 388 | tf_op jit(solution)/shard_map/while
  525.0 4.8 copy-start.9
  531.0 4.3 copy-start
  538.1 9.3 collective-permute-start.1
  561.7 12.2 %copy-start.6 = (f32[32]{0:T(128)}, f32[32]{0:T(128)S(1)}, u32[]{:S(2)}) copy-start(f32[32]{0:T(128)S(1)} %broadcast_multiply_fusion.4) | copy-start | bytes 388 | tf_op jit(solution)/shard_map/while
  561.9 4.8 copy-start.9
  567.8 4.3 copy-start
  575.0 9.3 collective-permute-start.1
  598.6 12.2 %copy-start.6 = (f32[32]{0:T(128)}, f32[32]{0:T(128)S(1)}, u32[]{:S(2)}) copy-start(f32[32]{0:T(128)S(1)} %broadcast_multiply_fusion.4) | copy-start | bytes 388 | tf_op jit(solution)/shard_map/while
  598.6 3.7 copy-start.7
  598.8 4.8 copy-start.9
  604.7 4.3 copy-start
  611.9 9.3 collective-permute-start.1
  635.4 12.2 %copy-start.6 = (f32[32]{0:T(128)}, f32[32]{0:T(128)S(1)}, u32[]{:S(2)}) copy-start(f32[32]{0:T(128)S(1)} %broadcast_multiply_fusion.4) | copy-start | bytes 388 | tf_op jit(solution)/shard_map/while
  635.7 4.8 copy-start.9
  641.6 4.3 copy-start
  648.8 9.3 collective-permute-start.1
  672.3 12.2 %copy-start.6 = (f32[32]{0:T(128)}, f32[32]{0:T(128)S(1)}, u32[]{:S(2)}) copy-start(f32[32]{0:T(128)S(1)} %broadcast_multiply_fusion.4) | copy-start | bytes 388 | tf_op jit(solution)/shard_map/while
  672.4 3.7 copy-start.7
  672.5 4.8 copy-start.9
  678.5 4.3 copy-start
  685.7 9.3 collective-permute-start.1
  709.2 12.2 %copy-start.6 = (f32[32]{0:T(128)}, f32[32]{0:T(128)S(1)}, u32[]{:S(2)}) copy-start(f32[32]{0:T(128)S(1)} %broadcast_multiply_fusion.4) | copy-start | bytes 388 | tf_op jit(solution)/shard_map/while
  709.4 4.8 copy-start.9
  715.4 4.3 copy-start
  722.6 9.3 collective-permute-start.1
  746.1 12.2 %copy-start.6 = (f32[32]{0:T(128)}, f32[32]{0:T(128)S(1)}, u32[]{:S(2)}) copy-start(f32[32]{0:T(128)S(1)} %broadcast_multiply_fusion.4) | copy-start | bytes 388 | tf_op jit(solution)/shard_map/while
  746.1 3.7 copy-start.7
  746.3 4.8 copy-start.9
  752.3 4.3 copy-start
  759.5 9.3 collective-permute-start.1
  (30 other events, 37.0 us)
Sparse Core Ops, SparseCore 0:
  795.0 133.3 reduce-scatter.3
where the time goes:
time: 950 us; the launch traced here: 938 us
  matrix products  322 us (34%)
  other arithmetic  208 us (22%)
  waiting for transfers between devices  183 us (19%)
  local copies, waits for them, and re-layouts  128 us (13%)
  starting transfers between devices  66.8 us (7%)
  loops' own time  17.1 us (2%)
  between operations  14.2 us (1%)
    unnamed x2, waiting for transfers between devices  134 us
    dot_general x33, matrix products, times_transposed(): lax.dot_general(left, right, (((1,), (1,)), ((), ())), preferred_element_...  119 us
    dynamic_update_slice x66, other arithmetic, place(): return lax.dynamic_update_index_in_dim(array, kept, slot, 0)  78.8 us
    ppermute x22, starting transfers between devices, shifted(): lax.ppermute(value, axis, [(source, source + steps) for source in range(f...  66.7 us
    ppermute x22, waiting for transfers between devices, shifted(): lax.ppermute(value, axis, [(source, source + steps) for source in range(f...  49.6 us
    dot_general x11, matrix products, layer_forward(): jnp.dot(normed, w_value, preferred_element_type=jnp.float32)  39 us
    dot_general x11, matrix products, layer_backward(): jnp.dot(grad_out, w_value, preferred_element_type=jnp.float32)  38.9 us
    dot_general x11, matrix products, layer_forward(): keys = jnp.dot(normed, w_key, preferred_element_type=jnp.float32)  38.8 us
  transfers between devices with their start and end apart: 23, of which 23 were waited for; matrix products, arithmetic and copies ran while one was open for 10% of the time, Pallas kernels for 0%

commit v1 on v0

v1 whole, which is shorter than its diff:
```python
import functools

import jax
import jax.numpy as jnp
from jax import lax
from jax.experimental import pallas as pl
from jax.experimental.pallas import tpu as pltpu
from jax.sharding import PartitionSpec as P

HD = 128
HEADS = 4
EPS = 1e-06
THETA = 1000000.0
SUB = 16
PIECES = 4
MESH = pl.DeviceIdType.MESH
F32 = jnp.float32
BF16 = jnp.bfloat16


def dot(left, right):
    return jnp.dot(left, right, preferred_element_type=F32)


def dot_t(left, right):
    return lax.dot_general(left, right, (((1,), (1,)), ((), ())), preferred_element_type=F32)


def t_dot(left, right):
    return lax.dot_general(left, right, (((0,), (0,)), ((), ())), preferred_element_type=F32)


def stack(array):
    return jnp.concatenate([array[:, h * HD : (h + 1) * HD] for h in range(HEADS)], axis=0)


def unstack(array):
    return jnp.concatenate([array[h * SUB : (h + 1) * SUB] for h in range(HEADS)], axis=1)


def swap(array):
    return pltpu.roll(array, HD // 2, 1)


def tall(array):
    return jnp.concatenate([array] * HEADS, axis=0)


def pipe_kernel(
    sections,
    x0,
    wk,
    wv,
    wscore,
    cosine,
    sine,
    mask,
    ends,
    target,
    hin,
    gin,
    gks,
    gvs,
    mixs,
    hout,
    gout,
    keys,
    values,
    probs,
    scales,
    scores,
    oscales,
    gweights,
    carry_v,
    carry_k,
    local_sem,
    hsend,
    hrecv,
    gsend,
    grecv,
):
    section = lax.axis_index("section")
    last = sections - 1
    chunks = hin.shape[0]
    model = hin.shape[2]
    piece = model // PIECES
    up = jnp.minimum(section + 1, last)
    down = jnp.maximum(section - 1, 0)

    barrier = pltpu.get_barrier_semaphore()

    @pl.when(section < last)
    def _():
        pl.semaphore_signal(barrier, inc=1, device_id={"section": up}, device_id_type=MESH)

    @pl.when(section > 0)
    def _():
        pl.semaphore_signal(barrier, inc=1, device_id={"section": down}, device_id_type=MESH)

    @pl.when(section == 0)
    def _():
        copy = pltpu.make_async_copy(x0, hin, local_sem)
        copy.start()
        copy.wait()

    keys[...] = jnp.zeros_like(keys)
    values[...] = jnp.zeros_like(values)

    @pl.when((section > 0) & (section < last))
    def _():
        pl.semaphore_wait(barrier, 2)

    @pl.when((section == 0) | (section == last))
    def _():
        pl.semaphore_wait(barrier, 1)

    def columns(p):
        return pl.ds(p * piece, piece)

    def h_copy(c, p):
        return pltpu.make_async_remote_copy(
            src_ref=hout.at[c, :, columns(p)],
            dst_ref=hin.at[c, :, columns(p)],
            send_sem=hsend.at[c, p],
            recv_sem=hrecv.at[c, p],
            device_id={"section": up},
            device_id_type=MESH,
        )

    def g_copy(c, p):
        return pltpu.make_async_remote_copy(
            src_ref=gout.at[c, :, columns(p)],
            dst_ref=gin.at[c, :, columns(p)],
            send_sem=gsend.at[c, p],
            recv_sem=grecv.at[c, p],
            device_id={"section": down},
            device_id_type=MESH,
        )

    def forward(c):
        row = c // 2
        acc_k = jnp.zeros((SUB, HEADS * HD), F32)
        acc_v = jnp.zeros((SUB, HEADS * HD), F32)
        square = jnp.zeros((SUB, 1), F32)
        for p in range(PIECES):

            @pl.when(section > 0)
            def _():
                h_copy(c, p).wait_recv()

            part = hin[c, :, columns(p)]
            acc_k += dot(part, wk[columns(p), :])
            acc_v += dot(part, wv[columns(p), :])
            full = part.astype(F32)
            square += jnp.sum(full * full, axis=1, keepdims=True)
        scale = lax.rsqrt(square / model + EPS)
        scales[c] = scale
        turned = stack(acc_k * scale)
        turned = turned * tall(cosine[c]) + swap(turned) * tall(sine[c])
        key = turned.astype(BF16)
        value = stack(acc_v * scale).astype(BF16)
        keys[c] = key
        values[c] = value
        all_keys = keys[pl.ds(row * 2, 2)].reshape(2 * HEADS * SUB, HD)
        all_values = values[pl.ds(row * 2, 2)].reshape(2 * HEADS * SUB, HD)
        logits = dot_t(key, all_keys) * (1.0 / HD)
        logits = jnp.where(mask[c] > 0.0, logits, -1e30)
        top = jnp.max(logits, axis=1, keepdims=True)
        expd = jnp.exp(logits - top)
        prob = expd / jnp.sum(expd, axis=1, keepdims=True)
        probs[c] = prob
        mixed = unstack(dot(prob.astype(BF16), all_values).astype(BF16))
        mixs[c] = mixed
        for p in range(PIECES):
            out = hin[c, :, columns(p)].astype(F32) + dot_t(mixed, wv[columns(p), :])
            hout[c, :, columns(p)] = out.astype(BF16)

            @pl.when(section < last)
            def _():
                h_copy(c, p).start()

        @pl.when(section == last)
        def _():
            square = jnp.zeros((SUB, 1), F32)
            score = jnp.zeros((SUB, 1), F32)
            for p in range(PIECES):
                full = hout[c, :, columns(p)].astype(F32)
                square += jnp.sum(full * full, axis=1, keepdims=True)
                score += jnp.sum(full * wscore[:, columns(p)], axis=1, keepdims=True)
            scale = lax.rsqrt(square / model + EPS)
            oscales[c] = scale
            scores[c] = score * scale

    def backward(j):
        row = j // 2
        half = 1 - lax.rem(j, 2)
        c = row * 2 + half

        @pl.when(section == last)
        def _():
            both = pl.ds(row * 2, 2)
            end = ends[both]
            score = scores[both]
            masked = jnp.where(end > 0.0, score, -1e30)
            top = jnp.max(jnp.max(masked, axis=0), axis=0, keepdims=True)
            expd = jnp.where(end > 0.0, jnp.exp(masked - top[None]), 0.0)
            total = jnp.sum(jnp.sum(expd, axis=0), axis=0, keepdims=True)
            gweights[...] = jnp.where(end > 0.0, expd / total[None] - target[both], 0.0)
            weight = gweights[half]
            scale = oscales[c]
            first = scale * weight
            second = scale * scale * weight * scores[c] * (1.0 / model)
            for p in range(PIECES):
                full = hout[c, :, columns(p)].astype(F32)
                gin[c, :, columns(p)] = (first * wscore[:, columns(p)] - second * full).astype(BF16)

        acc = jnp.zeros((SUB, HEADS * HD), F32)
        for p in range(PIECES):

            @pl.when(section < last)
            def _():
                g_copy(c, p).wait_recv()

            acc += dot(gin[c, :, columns(p)], wv[columns(p), :])
        scale = scales[c]
        grad_mixed = stack(acc).astype(BF16)
        all_keys = keys[pl.ds(row * 2, 2)].reshape(2 * HEADS * SUB, HD)
        all_values = values[pl.ds(row * 2, 2)].reshape(2 * HEADS * SUB, HD)
        key = keys[c]
        value = values[c]
        prob = probs[c]
        grad_probs = dot_t(grad_mixed, all_values)
        product = prob * grad_probs
        grad_scores = (product - prob * jnp.sum(product, axis=1, keepdims=True)).astype(BF16)
        from_v = t_dot(prob.astype(BF16), grad_mixed)
        from_k = t_dot(grad_scores, key)
        lower = HEADS * SUB
        second = half == 1
        own_v = jnp.where(second, from_v[lower:], from_v[:lower] + carry_v[...])
        own_k = jnp.where(second, from_k[lower:], from_k[:lower] + carry_k[...])
        carry_v[...] = from_v[:lower]
        carry_k[...] = from_k[:lower]
        turned = (dot(grad_scores, all_keys) + own_k) * (1.0 / HD)
        grad_value = own_v.astype(BF16)
        along = jnp.sum(turned * key.astype(F32) + own_v * value.astype(F32), axis=1, keepdims=True)
        along = along[:SUB] + along[SUB : 2 * SUB] + along[2 * SUB : 3 * SUB] + along[3 * SUB :]
        along = along * (scale * scale) * (1.0 / model)
        grad_key = (turned * tall(cosine[c]) - swap(turned) * tall(sine[c])).astype(BF16)
        flat_key = unstack(grad_key)
        flat_value = unstack(grad_value)
        gks[c] = (flat_key.astype(F32) * scale).astype(BF16)
        gvs[c] = (flat_value.astype(F32) * scale).astype(BF16)

        @pl.when(section > 0)
        def _():
            for p in range(PIECES):
                grad = dot_t(flat_key, wk[columns(p), :]) + dot_t(flat_value, wv[columns(p), :])
                out = (
                    gin[c, :, columns(p)].astype(F32)
                    + scale * grad
                    - along * hin[c, :, columns(p)].astype(F32)
                )
                gout[c, :, columns(p)] = out.astype(BF16)
                g_copy(c, p).start()

    lead = jnp.where(section == last, 1, jnp.where(section == last - 1, 5, chunks))

    def slot(i, unused):
        @pl.when(i < chunks)
        def _():
            forward(i)

        j = i - lead

        @pl.when((j >= 0) & (j < chunks))
        def _():
            backward(j)

        return unused

    lax.fori_loop(0, 2 * chunks, slot, 0)

    def drain(c, unused):
        for p in range(PIECES):

            @pl.when(section < last)
            def _():
                h_copy(c, p).wait_send()

            @pl.when(section > 0)
            def _():
                g_copy(c, p).wait_send()

        return unused

    lax.fori_loop(0, chunks, drain, 0)


def tables(segments, lengths, grades):
    micro, width = segments.shape
    index = jnp.arange(width, dtype=jnp.int32)
    change = segments[:, 1:] != segments[:, :-1]
    starts = jnp.concatenate([jnp.ones((micro, 1), bool), change], axis=1)
    same = segments[:, :, None] == segments[:, None, :]
    first = jnp.max(jnp.where(starts[:, None, :] & (index[None, :] <= index[:, None]), index, 0), axis=2)
    offset = (index - first).astype(F32)
    freqs = THETA ** (-(jnp.arange(HD // 2, dtype=F32) * 2.0) / HD)
    angles = offset[..., None] * freqs
    cosine, sine = jnp.cos(angles), jnp.sin(angles)
    chunks = micro * width // SUB
    cosine = jnp.concatenate([cosine, cosine], axis=-1).reshape(chunks, SUB, HD)
    sine = jnp.concatenate([-sine, sine], axis=-1).reshape(chunks, SUB, HD)
    live = index < lengths
    causal = index[None, :] <= index[:, None]
    allowed = same & causal & live[:, :, None] & live[:, None, :]
    allowed = allowed | jnp.eye(width, dtype=bool)
    halves = width // SUB
    allowed = allowed.reshape(micro, halves, 1, SUB, halves, 1, SUB)
    heads = jnp.eye(HEADS, dtype=bool).reshape(1, 1, HEADS, 1, 1, HEADS, 1)
    mask = (allowed & heads).astype(F32).reshape(chunks, HEADS * SUB, halves * HEADS * SUB)
    following = jnp.concatenate([change, jnp.ones((micro, 1), bool)], axis=1)
    ends = live & (following | (index == lengths - 1))
    target = jax.nn.softmax(jnp.where(ends, grades.astype(F32), -1e30), axis=-1)
    ends = ends.astype(F32).reshape(chunks, SUB, 1)
    target = target.reshape(chunks, SUB, 1)
    return cosine, sine, mask, ends, target


def over_tokens(left, right):
    return t_dot(left, right)


def shards(x0, w_key, w_value, w_score, segments, lengths, grades):
    sections = lax.axis_size("section")
    micro, width, model = x0.shape
    features = w_key.shape[2]
    chunks = micro * width // SUB
    cosine, sine, mask, ends, target = tables(segments, lengths, grades)
    vmem = pl.BlockSpec(memory_space=pltpu.VMEM)
    act = (chunks, SUB, model)
    flat = (chunks, SUB, features)
    stacked = (chunks, HEADS * SUB, HD)
    hin, gin, gks, gvs, mixs = pl.pallas_call(
        functools.partial(pipe_kernel, sections),
        out_shape=[jax.ShapeDtypeStruct(s, BF16) for s in (act, act, flat, flat, flat)],
        in_specs=[pl.BlockSpec(memory_space=pl.ANY)] + [vmem] * 8,
        out_specs=[vmem] * 5,
        scratch_shapes=[
            pltpu.VMEM(act, BF16),
            pltpu.VMEM(act, BF16),
            pltpu.VMEM(stacked, BF16),
            pltpu.VMEM(stacked, BF16),
            pltpu.VMEM((chunks, HEADS * SUB, 2 * HEADS * SUB), F32),
            pltpu.VMEM((chunks, SUB, 1), F32),
            pltpu.VMEM((chunks, SUB, 1), F32),
            pltpu.VMEM((chunks, SUB, 1), F32),
            pltpu.VMEM((2, SUB, 1), F32),
            pltpu.VMEM((HEADS * SUB, HD), F32),
            pltpu.VMEM((HEADS * SUB, HD), F32),
            pltpu.SemaphoreType.DMA,
            pltpu.SemaphoreType.DMA((chunks, PIECES)),
            pltpu.SemaphoreType.DMA((chunks, PIECES)),
            pltpu.SemaphoreType.DMA((chunks, PIECES)),
            pltpu.SemaphoreType.DMA((chunks, PIECES)),
        ],
        compiler_params=pltpu.CompilerParams(
            collective_id=0, has_side_effects=True, vmem_limit_bytes=48 * 2**20
        ),
    )(
        x0.reshape(act),
        w_key[0],
        w_value[0],
        w_score.reshape(1, model),
        cosine,
        sine,
        mask,
        ends,
        target,
    )
    tokens = micro * width
    hidden = hin.reshape(tokens, model)
    grads = gin.reshape(tokens, model)
    part_key = over_tokens(hidden, gks.reshape(tokens, features))
    part_value = over_tokens(hidden, gvs.reshape(tokens, features)) + over_tokens(
        grads, mixs.reshape(tokens, features)
    )
    summed = lax.psum_scatter(
        jnp.concatenate([part_key, part_value], axis=1).astype(BF16),
        "dp",
        scatter_dimension=0,
        tiled=True,
    ).astype(F32)
    return (summed[None, :, :features], summed[None, :, features:])


def solution(mesh):
    placed = (
        P(None, "dp", None),
        P("section", None, None),
        P("section", None, None),
        P(),
        P(None, "dp"),
        P(None, "dp"),
        P(None, "dp"),
    )
    return jax.shard_map(
        shards,
        mesh=mesh,
        in_specs=placed,
        out_specs=(P("section", "dp", None), P("section", "dp", None)),
        check_vma=False,
    )
```

time: 950 us -> 333 us (0.35); the launches traced: 938 us -> 333 us
  matrix products: 322 us -> 4.75 us
  other arithmetic: 208 us -> 10.6 us
  Pallas kernels: 0 us -> 171 us
  local copies, waits for them, and re-layouts: 128 us -> 22.1 us
  waiting for transfers between devices: 183 us -> 110 us
  starting transfers between devices: 66.8 us -> 0.04 us
  loops' own time: 17.1 us -> 0 us
    dot_general x146 -> x3, matrix products: 296 us -> 4.75 us  [t_dot(): lax.dot_general(left, right, (((0,), (0,)), ((), ())), preferred_element_...]
    pallas_call x0 -> x1, Pallas kernels: none -> 171 us  [shards(): pl.pallas_call(functools.partial(pipe_kernel, sections), out_shape=[jax.S...]
    dynamic_update_slice x66 -> x0, other arithmetic: 78.8 us -> none  [place(): return lax.dynamic_update_index_in_dim(array, kept, slot, 0)]
    ppermute x22 -> x0, starting transfers between devices: 66.7 us -> none  [shifted(): lax.ppermute(value, axis, [(source, source + steps) for source in range(f...]
    dynamic_slice x55 -> x0, local copies, waits for them, and re-layouts: 53.7 us -> none  [the longest x22 26.8 us: shards(): lax.scan(forward_tick, start, jnp.arange(ticks, dtype=jnp.int32))]
    ppermute x22 -> x0, waiting for transfers between devices: 49.6 us -> none  [shifted(): lax.ppermute(value, axis, [(source, source + steps) for source in range(f...]
    reduce_sum x56 -> x1, other arithmetic: 34.1 us -> 0.87 us  [tables(): jax.nn.softmax(jnp.where(ends, grades.astype(F32), -1e+30), axis=-1)]
    reduce_max x11 -> x2, other arithmetic: 28.9 us -> 1.02 us  [the longest x1 0.87 us: tables(): jax.nn.softmax(jnp.where(ends, grades.astype(F32), -1e+30), axis=-1)]
  transfers between devices with their start and end apart: 23 -> 1, of which waited for: 23 -> 1; matrix products, arithmetic and copies ran while one was open for 10% -> 0% of each run, Pallas kernels for 0% -> 0%
where the time goes in v1:
time: 333 us
  Pallas kernels  171 us (51%)
  waiting for transfers between devices  110 us (33%)
  local copies, waits for them, and re-layouts  22.1 us (7%)
  between operations  14.2 us (4%)
  other arithmetic  10.6 us (3%)
  matrix products  4.75 us (1%)
    pallas_call x1, Pallas kernels, shards(): pl.pallas_call(functools.partial(pipe_kernel, sections), out_shape=[jax.S...  171 us
    unnamed x2, waiting for transfers between devices  110 us
    unnamed x8, local copies, waits for them, and re-layouts  19.4 us
  transfers between devices with their start and end apart: 1, of which 1 were waited for; matrix products, arithmetic and copies ran while one was open for 0% of the time, Pallas kernels for 0%

profile of v1, /device:TPU:1, one launch (start us, length us, event | category | flops | bytes accessed | tf_op | source)
XLA Modules:
  0.0 332.5 jit_solution(6499305795475419860)
XLA Ops:
  7.2 0.0 reduce-scatter.4.cloned.1.call-start
  7.2 0.8 slice_compare_fusion
  8.1 0.8 eq.46
  8.9 0.7 add_bitcast_fusion
  9.5 0.1 broadcast_compare_fusion.1
  9.6 0.7 broadcast_compare_fusion.2
  10.4 0.9 fusion.6
  11.2 0.9 fusion.5
  12.1 0.8 fusion.4
  12.9 0.1 reshape.174.target
  13.0 0.1 concatenate.18
  13.1 0.2 select_reduce_fusion
  13.2 0.1 reduce_max.21
  13.3 0.3 and_or_fusion
  13.6 0.5 and.81
  14.1 0.7 and.82
  14.8 0.1 and.83
  14.9 0.1 and.84
  15.1 0.1 reshape.173.ends
  15.2 0.3 fusion.1
  15.6 0.1 pad_maximum_fusion.1
  15.7 0.0 copy-start
  15.7 1.3 copy-done
  17.0 0.0 copy-start.1
  17.0 0.7 copy-done.1
  17.7 171.0 %shard_map.89 = (bf16[8,16,5120]{2,1,0:T(8,128)(2,1)S(1)}, bf16[8,16,5120]{2,1,0:T(8,128)(2,1)S(1)}, bf16[8,16,512]{2,1,0:T(8,128)(2,1)S(1)}, bf16[8,16,512]{2,1,0:T(8,128)(2,1)S(1)}, bf16[8,16,512]{2,1,0:T(8,128)(2,1)S(1)}) custom-call(bf16[8,16,5120]{2,1,0:T(8,128)(2,1)S(1)} %bitcast.27, bf16[5120,512]{1,0:T(8,128)(2,1)} %bitcast.29, ...), custom_call_target="tpu_custom_call" | custom-call | tf_op jit(solution)/shard_map/pallas_call | solution.py:343
  188.8 1.6 fusion.8
  190.3 1.6 bitcast_convert_fusion
  191.9 1.6 fusion
  193.5 4.8 %pad_maximum_fusion = bf16[5120,1024]{0,1:T(8,128)(2,1)} fusion(bf16[5120,512]{0,1:T(8,128)(2,1)S(1)} %fusion, bf16[5120,512]{0,1:T(8,128)(2,1)S(1)} %bitcast_convert_fusion), kind=kLoop, calls=%fused_computation | loop fusion | flops 20971520 | bytes 20971520 | tf_op jit(solution)/shard_map/concatenate | solution.py:388
  198.3 14.4 %copy.21 = bf16[5120,1024]{1,0:T(8,128)(2,1)} copy(bf16[5120,1024]{0,1:T(8,128)(2,1)} %pad_maximum_fusion) | data formatting | bytes 20971520
  212.7 0.0 reduce-scatter.4.cloned.1.call-update
  212.7 109.8 %reduce-scatter.4.cloned.1.call-done = bf16[160,1024]{1,0:T(8,128)(2,1)} async-done(((bf16[5120,1024]{1,0:T(8,128)(2,1)}), bf16[160,1024]{1,0:T(8,128)(2,1)}) %reduce-scatter.4.cloned.1.call-update) | async-done | bytes 327696
  322.6 1.2 copy.22
  323.7 0.1 convert_element_type.22
  323.8 0.1 slice_bitcast_fusion
  323.9 0.9 copy.19
  324.8 0.9 copy.20
  (8 shorter events, 0.1 us)
Async XLA Ops:
  7.2 315.4 %reduce-scatter.4.cloned.1.call-start = ((), (), s32[]{:S(2)}) async-start(), calls=%async_computation.1 | async-start | bytes 10813440
  15.7 1.3 copy-start
  17.0 0.7 copy-start.1
Sparse Core Ops, SparseCore 0:
  212.9 109.6 reduce-scatter.3

commit v2 on v1

--- a/solution.py
+++ b/solution.py
@@ -57,10 +57,11 @@
     mask,
     ends,
     target,
+    out_key,
+    out_value,
     hin,
     gin,
-    gks,
-    gvs,
+    gkv,
     mixs,
     hout,
     gout,
@@ -73,13 +74,40 @@
     gweights,
     carry_v,
     carry_k,
+    peer_h,
+    peer_g,
+    peer_gkv,
+    peer_mix,
+    total,
+    pair_out,
+    pair_in,
+    first_out,
+    first_in,
+    second_out,
+    second_in,
     local_sem,
     hsend,
     hrecv,
     gsend,
     grecv,
+    xsend,
+    xrecv,
+    pair_send,
+    pair_recv,
+    first_send,
+    first_recv,
+    second_send,
+    second_recv,
 ):
     section = lax.axis_index("section")
+    place = lax.axis_index("dp")
+    x, y, core = place // 8, (place // 2) % 4, place % 2
+    xpeers = [((x + r) % 4) * 8 + place % 8 for r in range(1, 4)]
+    sibling = x * 8 + y * 2 + (1 - core)
+    beside = y + 1 - 2 * (y % 2)
+    across = 3 - y
+    opposite = (y + 2) % 4
+    ydevices = [x * 8 + beside * 2 + core, x * 8 + across * 2 + core]
     last = sections - 1
     chunks = hin.shape[0]
     model = hin.shape[2]
@@ -106,13 +134,16 @@
     keys[...] = jnp.zeros_like(keys)
     values[...] = jnp.zeros_like(values)
 
+    for peer in xpeers + ydevices + [sibling]:
+        pl.semaphore_signal(barrier, inc=1, device_id={"dp": peer}, device_id_type=MESH)
+
     @pl.when((section > 0) & (section < last))
     def _():
-        pl.semaphore_wait(barrier, 2)
+        pl.semaphore_wait(barrier, 8)
 
     @pl.when((section == 0) | (section == last))
     def _():
-        pl.semaphore_wait(barrier, 1)
+        pl.semaphore_wait(barrier, 7)
 
     def columns(p):
         return pl.ds(p * piece, piece)
@@ -134,6 +165,23 @@
             send_sem=gsend.at[c, p],
             recv_sem=grecv.at[c, p],
             device_id={"section": down},
+            device_id_type=MESH,
+        )
+
+    def x_copy(kind, c, r):
+        peer = (x + r) % 4
+        source, target = (
+            (hin.at[c, :, pl.ds(pl.multiple_of(peer * piece, 128), piece)], peer_h),
+            (mixs.at[c], peer_mix),
+            (gin.at[c, :, pl.ds(pl.multiple_of(peer * piece, 128), piece)], peer_g),
+            (gkv.at[c], peer_gkv),
+        )[kind]
+        return pltpu.make_async_remote_copy(
+            src_ref=source,
+            dst_ref=target.at[r - 1, c],
+            send_sem=xsend.at[kind, c, r - 1],
+            recv_sem=xrecv.at[kind, c, r - 1],
+            device_id={"dp": xpeers[r - 1]},
             device_id_type=MESH,
         )
 
@@ -178,6 +226,10 @@
             @pl.when(section < last)
             def _():
                 h_copy(c, p).start()
+
+        for r in range(1, 4):
+            x_copy(0, c, r).start()
+            x_copy(1, c, r).start()
 
         @pl.when(section == last)
         def _():
@@ -248,8 +300,9 @@
         grad_key = (turned * tall(cosine[c]) - swap(turned) * tall(sine[c])).astype(BF16)
         flat_key = unstack(grad_key)
         flat_value = unstack(grad_value)
-        gks[c] = (flat_key.astype(F32) * scale).astype(BF16)
-        gvs[c] = (flat_value.astype(F32) * scale).astype(BF16)
+        features = HEADS * HD
+        gkv[c, :, :features] = (flat_key.astype(F32) * scale).astype(BF16)
+        gkv[c, :, features:] = (flat_value.astype(F32) * scale).astype(BF16)
 
         @pl.when(section > 0)
         def _():
@@ -263,6 +316,117 @@
                 gout[c, :, columns(p)] = out.astype(BF16)
                 g_copy(c, p).start()
 
+        for r in range(1, 4):
+            x_copy(2, c, r).start()
+            x_copy(3, c, r).start()
+
+    tile = 256
+    group = chunks // 2
+
+    def weights(base, again):
+        def arrive(c, unused):
+            for kind in range(4):
+                for r in range(1, 4):
+                    x_copy(kind, base + c, r).wait_recv()
+            return unused
+
+        lax.fori_loop(0, group, arrive, 0)
+        which = pl.ds(base, group)
+
+        def gather(own, peers):
+            own = own.reshape(group * SUB, own.shape[-1])
+            peers = peers.reshape(3 * group * SUB, peers.shape[-1])
+            return jnp.concatenate([own, peers], axis=0)
+
+        def block(t, unused):
+            there = pl.ds(pl.multiple_of(t * tile, tile), tile)
+            mine = pl.ds(pl.multiple_of(x * piece + t * tile, 128), tile)
+            hidden = gather(hin[which, :, mine], peer_h[:, which, :, there])
+            grads = gather(gin[which, :, mine], peer_g[:, which, :, there])
+            both = gather(gkv[which], peer_gkv[:, which])
+            mixed = gather(mixs[which], peer_mix[:, which])
+            features = HEADS * HD
+            part_key = t_dot(hidden, both[:, :features])
+            part_value = t_dot(hidden, both[:, features:]) + t_dot(grads, mixed)
+            if again:
+                part_key = part_key + total[there, :features]
+                part_value = part_value + total[there, features:]
+            total[there, :features] = part_key
+            total[there, features:] = part_value
+            return unused
+
+        lax.fori_loop(0, piece // tile, block, 0)
+
+    share = piece // 8
+    half_features = HEADS * HD
+    sides = [pl.ds(0, half_features), pl.ds(half_features, half_features)]
+
+    def rows_of(ypart, corepart):
+        return pl.ds(pl.multiple_of((ypart * 2 + corepart) * share, 32), share)
+
+    def pair_copy(k):
+        return pltpu.make_async_remote_copy(
+            src_ref=pair_out.at[k],
+            dst_ref=pair_in.at[k],
+            send_sem=pair_send.at[k],
+            recv_sem=pair_recv.at[k],
+            device_id={"dp": sibling},
+            device_id_type=MESH,
+        )
+
+    def first_copy(side, k):
+        return pltpu.make_async_remote_copy(
+            src_ref=first_out.at[side, k],
+            dst_ref=first_in.at[side, k],
+            send_sem=first_send.at[side, k],
+            recv_sem=first_recv.at[side, k],
+            device_id={"dp": ydevices[side]},
+            device_id_type=MESH,
+        )
+
+    def second_copy(side):
+        return pltpu.make_async_remote_copy(
+            src_ref=second_out.at[side],
+            dst_ref=second_in.at[side],
+            send_sem=second_send.at[side],
+            recv_sem=second_recv.at[side],
+            device_id={"dp": ydevices[1 - side]},
+            device_id_type=MESH,
+        )
+
+    def scatter():
+        order = [opposite, beside, across, y]
+        for k in range(4):
+            pair_out[k] = total[rows_of(order[k], 1 - core), :].astype(BF16)
+            pair_copy(k).start()
+
+        def held(k, side):
+            return total[rows_of(order[k], core), sides[side]] + pair_in[k, :, sides[side]].astype(F32)
+
+        pair_copy(0).wait_recv()
+        for side in range(2):
+            first_out[side, 1] = held(0, side).astype(BF16)
+            first_copy(side, 1).start()
+        for side in range(2):
+            pair_copy(1 + side).wait_recv()
+            first_out[side, 0] = held(1 + side, side).astype(BF16)
+            first_copy(side, 0).start()
+        for side in range(2):
+            first_copy(side, 1).wait_recv()
+            second_out[side] = (held(2 - side, side) + first_in[side, 1].astype(F32)).astype(BF16)
+            second_copy(side).start()
+        pair_copy(3).wait_recv()
+        for side, out in ((0, out_key), (1, out_value)):
+            first_copy(side, 0).wait_recv()
+            second_copy(side).wait_recv()
+            out[...] = held(3, side) + first_in[side, 0].astype(F32) + second_in[side].astype(F32)
+        for k in range(4):
+            pair_copy(k).wait_send()
+        for side in range(2):
+            first_copy(side, 0).wait_send()
+            first_copy(side, 1).wait_send()
+            second_copy(side).wait_send()
+
     lead = jnp.where(section == last, 1, jnp.where(section == last - 1, 5, chunks))
 
     def slot(i, unused):
@@ -276,9 +440,15 @@
         def _():
             backward(j)
 
+        @pl.when(j == group + 1)
+        def _():
+            weights(0, False)
+
         return unused
 
     lax.fori_loop(0, 2 * chunks, slot, 0)
+    weights(group, True)
+    scatter()
 
     def drain(c, unused):
         for p in range(PIECES):
@@ -291,6 +461,9 @@
             def _():
                 g_copy(c, p).wait_send()
 
+        for kind in range(4):
+            for r in range(1, 4):
+                x_copy(kind, c, r).wait_send()
         return unused
 
     lax.fori_loop(0, chunks, drain, 0)
@@ -326,10 +499,6 @@
     return cosine, sine, mask, ends, target
 
 
-def over_tokens(left, right):
-    return t_dot(left, right)
-
-
 def shards(x0, w_key, w_value, w_score, segments, lengths, grades):
     sections = lax.axis_size("section")
     micro, width, model = x0.shape
@@ -340,12 +509,19 @@
     act = (chunks, SUB, model)
     flat = (chunks, SUB, features)
     stacked = (chunks, HEADS * SUB, HD)
-    hin, gin, gks, gvs, mixs = pl.pallas_call(
+    piece = model // PIECES
+    share = piece // 8
+    dma = pltpu.SemaphoreType.DMA
+    grad_key, grad_value = pl.pallas_call(
         functools.partial(pipe_kernel, sections),
-        out_shape=[jax.ShapeDtypeStruct(s, BF16) for s in (act, act, flat, flat, flat)],
+        out_shape=[jax.ShapeDtypeStruct((share, features), F32)] * 2,
         in_specs=[pl.BlockSpec(memory_space=pl.ANY)] + [vmem] * 8,
-        out_specs=[vmem] * 5,
+        out_specs=[vmem] * 2,
         scratch_shapes=[
+            pltpu.VMEM(act, BF16),
+            pltpu.VMEM(act, BF16),
+            pltpu.VMEM((chunks, SUB, 2 * features), BF16),
+            pltpu.VMEM(flat, BF16),
             pltpu.VMEM(act, BF16),
             pltpu.VMEM(act, BF16),
             pltpu.VMEM(stacked, BF16),
@@ -357,14 +533,33 @@
             pltpu.VMEM((2, SUB, 1), F32),
             pltpu.VMEM((HEADS * SUB, HD), F32),
             pltpu.VMEM((HEADS * SUB, HD), F32),
-            pltpu.SemaphoreType.DMA,
-            pltpu.SemaphoreType.DMA((chunks, PIECES)),
-            pltpu.SemaphoreType.DMA((chunks, PIECES)),
-            pltpu.SemaphoreType.DMA((chunks, PIECES)),
-            pltpu.SemaphoreType.DMA((chunks, PIECES)),
+            pltpu.VMEM((3, chunks, SUB, piece), BF16),
+            pltpu.VMEM((3, chunks, SUB, piece), BF16),
+            pltpu.VMEM((3, chunks, SUB, 2 * features), BF16),
+            pltpu.VMEM((3, chunks, SUB, features), BF16),
+            pltpu.VMEM((piece, 2 * features), F32),
+            pltpu.VMEM((4, share, 2 * features), BF16),
+            pltpu.VMEM((4, share, 2 * features), BF16),
+            pltpu.VMEM((2, 2, share, features), BF16),
+            pltpu.VMEM((2, 2, share, features), BF16),
+            pltpu.VMEM((2, share, features), BF16),
+            pltpu.VMEM((2, share, features), BF16),
+            dma,
+            dma((chunks, PIECES)),
+            dma((chunks, PIECES)),
+            dma((chunks, PIECES)),
+            dma((chunks, PIECES)),
+            dma((4, chunks, 3)),
+            dma((4, chunks, 3)),
+            dma((4,)),
+            dma((4,)),
+            dma((2, 2)),
+            dma((2, 2)),
+            dma((2,)),
+            dma((2,)),
         ],
         compiler_params=pltpu.CompilerParams(
-            collective_id=0, has_side_effects=True, vmem_limit_bytes=48 * 2**20
+            collective_id=0, has_side_effects=True, vmem_limit_bytes=56 * 2**20
         ),
     )(
         x0.reshape(act),
@@ -377,20 +572,7 @@
         ends,
         target,
     )
-    tokens = micro * width
-    hidden = hin.reshape(tokens, model)
-    grads = gin.reshape(tokens, model)
-    part_key = over_tokens(hidden, gks.reshape(tokens, features))
-    part_value = over_tokens(hidden, gvs.reshape(tokens, features)) + over_tokens(
-        grads, mixs.reshape(tokens, features)
-    )
-    summed = lax.psum_scatter(
-        jnp.concatenate([part_key, part_value], axis=1).astype(BF16),
-        "dp",
-        scatter_dimension=0,
-        tiled=True,
-    ).astype(F32)
-    return (summed[None, :, :features], summed[None, :, features:])
+    return (grad_key[None], grad_value[None])
 
 
 def solution(mesh):

time: 333 us -> 225 us (0.68)
  waiting for transfers between devices: 110 us -> 0 us
  Pallas kernels: 171 us -> 209 us
  local copies, waits for them, and re-layouts: 22.1 us -> 7.24 us
  between operations: 14.2 us -> 0.71 us
  matrix products: 4.75 us -> 0 us
  other arithmetic: 10.6 us -> 7.15 us
    unnamed x2 -> x0, waiting for transfers between devices: 110 us -> none
    pallas_call x1, Pallas kernels: 171 us -> 209 us  [shards(): pl.pallas_call(functools.partial(pipe_kernel, sections), out_shape=[jax.S...]
    unnamed x8 -> x2, local copies, waits for them, and re-layouts: 19.4 us -> 3.44 us
    concatenate x1 -> x0, other arithmetic: 4.78 us -> none  [shards(): jnp.concatenate([part_key, part_value], axis=1).astype(BF16)]
    dot_general x3 -> x0, matrix products: 4.75 us -> none  [t_dot(): lax.dot_general(left, right, (((0,), (0,)), ((), ())), preferred_element_...]
  transfers between devices with their start and end apart: 1 -> 0, of which waited for: 1 -> 0; matrix products, arithmetic and copies ran while one was open for 0% -> 0% of each run, Pallas kernels for 0% -> 0%
where the time goes in v2:
time: 225 us; the launch traced here: 224 us
  Pallas kernels  209 us (93%)
  local copies, waits for them, and re-layouts  7.24 us (3%)
  other arithmetic  7.15 us (3%)
    pallas_call x1, Pallas kernels, shards(): pl.pallas_call(functools.partial(pipe_kernel, sections), out_shape=[jax.S...  209 us

profile of v2, /device:TPU:1, one launch (start us, length us, event | category | flops | bytes accessed | tf_op | source)
XLA Modules:
  0.0 224.2 jit_solution(9967560805086719550)
XLA Ops:
  0.6 0.8 slice_compare_fusion
  1.5 0.1 concatenate.14
  1.5 0.7 add_bitcast_fusion
  2.2 0.9 fusion.5
  3.1 0.9 fusion.4
  4.0 0.8 fusion.3
  4.7 0.7 broadcast_compare_fusion.2
  5.5 0.8 eq.46
  6.2 0.2 select_reduce_fusion
  6.4 0.1 reduce_max.21
  6.5 0.1 broadcast_compare_fusion.1
  6.6 0.3 and_or_fusion
  6.9 0.7 reshape.165.ends
  7.7 0.7 reshape.166.target
  8.4 0.1 and.83
  8.5 0.1 and.84
  8.7 0.3 fusion
  9.0 0.7 pad_maximum_fusion
  9.7 0.5 and.81
  10.2 0.7 and.82
  10.9 0.7 and_convert_fusion.mask
  11.7 209.1 %shard_map.89 = (f32[160,512]{1,0:T(8,128)}, f32[160,512]{1,0:T(8,128)}) custom-call(bf16[8,16,5120]{2,1,0:T(8,128)(2,1)} %bitcast.12, bf16[5120,512]{1,0:T(8,128)(2,1)} %bitcast.10, bf16[5120,512]{1,0:T(8,128)(2,1)} %bitcast.11, f32[1,5120]{1,0:T(1,128)} %bitcast.15, f32[8,16,128]{2,1,0:T(8,128)} %get-tuple-element.13.cosine, ...), custom_call_target="tpu_custom_call" | custom-call | tf_op jit(solution)/shard_map/pallas_call | solution.py:515
  220.7 1.7 copy.15
  222.5 1.7 copy.16
  (7 shorter events, 0.0 us)

commit v3 on v2

v3 whole, which is shorter than its diff:
```python
import functools
import math

import jax
import jax.numpy as jnp
from jax import lax
from jax.experimental import pallas as pl
from jax.experimental.pallas import tpu as pltpu
from jax.sharding import PartitionSpec as P

HD = 128
HEADS = 4
EPS = 1e-06
THETA = 1000000.0
SUB = 16
PIECES = 4
MESH = pl.DeviceIdType.MESH
F32 = jnp.float32
BF16 = jnp.bfloat16


def dot(left, right):
    return jnp.dot(left, right, preferred_element_type=F32)


def dot_t(left, right):
    return lax.dot_general(left, right, (((1,), (1,)), ((), ())), preferred_element_type=F32)


def t_dot(left, right):
    return lax.dot_general(left, right, (((0,), (0,)), ((), ())), preferred_element_type=F32)


def stack(array):
    blocks = []
    for start in range(0, array.shape[0], SUB):
        blocks += [array[start : start + SUB, h * HD : (h + 1) * HD] for h in range(HEADS)]
    return jnp.concatenate(blocks, axis=0)


def unstack(array):
    rows = []
    for start in range(0, array.shape[0], HEADS * SUB):
        blocks = [array[start + h * SUB : start + (h + 1) * SUB] for h in range(HEADS)]
        rows.append(jnp.concatenate(blocks, axis=1))
    return jnp.concatenate(rows, axis=0)


def swap(array):
    return pltpu.roll(array, HD // 2, 1)


def tall(array):
    return jnp.concatenate([array[k] for k in range(array.shape[0]) for h in range(HEADS)], axis=0)


def pipe_kernel(
    sections,
    x0,
    wk_all,
    wv_all,
    wscore,
    segments,
    lengths,
    grades,
    out_key,
    out_value,
    wk,
    wv,
    wkt,
    wvt,
    slots,
    cosine,
    sine,
    mask,
    ends,
    levels,
    hin,
    gin,
    gkv,
    mixs,
    hout,
    gout,
    keys,
    values,
    probs,
    scales,
    carry_v,
    carry_k,
    peer_h,
    peer_g,
    peer_gkv,
    peer_mix,
    total,
    pair_out,
    pair_in,
    first_out,
    first_in,
    second_out,
    second_in,
    local_sem,
    weight_sem,
    hsend,
    hrecv,
    gsend,
    grecv,
    xsend,
    xrecv,
    pair_send,
    pair_recv,
    first_send,
    first_recv,
    second_send,
    second_recv,
):
    section = lax.axis_index("section")
    place = lax.axis_index("dp")
    x, y, core = place // 8, (place // 2) % 4, place % 2
    xpeers = [((x + r) % 4) * 8 + place % 8 for r in range(1, 4)]
    sibling = x * 8 + y * 2 + (1 - core)
    beside = y + 1 - 2 * (y % 2)
    across = 3 - y
    opposite = (y + 2) % 4
    ydevices = [x * 8 + beside * 2 + core, x * 8 + across * 2 + core]
    last = sections - 1
    chunks = hin.shape[0]
    model = hin.shape[2]
    piece = model // PIECES
    up = jnp.minimum(section + 1, last)
    down = jnp.maximum(section - 1, 0)

    rows = HEADS * SUB
    load_k = pltpu.make_async_copy(wk_all, wk, weight_sem.at[0])
    load_v = pltpu.make_async_copy(wv_all, wv, weight_sem.at[1])
    load_x = pltpu.make_async_copy(x0, hin, local_sem)
    load_k.start()
    load_v.start()

    @pl.when(section == 0)
    def _():
        load_x.start()

    barrier = pltpu.get_barrier_semaphore()

    @pl.when(section < last)
    def _():
        pl.semaphore_signal(barrier, inc=1, device_id={"section": up}, device_id_type=MESH)

    @pl.when(section > 0)
    def _():
        pl.semaphore_signal(barrier, inc=1, device_id={"section": down}, device_id_type=MESH)

    for peer in xpeers + ydevices + [sibling]:
        pl.semaphore_signal(barrier, inc=1, device_id={"dp": peer}, device_id_type=MESH)

    keys[...] = jnp.zeros_like(keys)
    values[...] = jnp.zeros_like(values)
    source = lax.broadcasted_iota(jnp.int32, (slots.shape[0] * 4, 2 * rows), 0)
    lane = lax.broadcasted_iota(jnp.int32, (slots.shape[0] * 4, 2 * rows), 1)
    spread = (source == (lane // rows) * SUB + lane % SUB).astype(BF16)
    both = jnp.concatenate([segments[...], grades[...]], axis=0).astype(F32).astype(BF16)
    slots[...] = dot(both, spread)

    def make_tables(c, unused):
        row, half = c // 2, lax.rem(c, 2)
        sub = lax.broadcasted_iota(jnp.int32, (rows, 2 * rows), 0)
        lane = lax.broadcasted_iota(jnp.int32, (rows, 2 * rows), 1)
        slot_i = half * SUB + sub % SUB
        slot_j = (lane // rows) * SUB + lane % SUB
        seg_j = jnp.broadcast_to(slots[pl.ds(row, 1), :], (rows, 2 * rows))
        grade_j = jnp.broadcast_to(slots[pl.ds(row + chunks // 2, 1), :], (rows, 2 * rows))
        here = lane == half * rows + sub
        seg_i = jnp.sum(jnp.where(here, seg_j, 0.0), axis=1, keepdims=True)
        grade_i = jnp.sum(jnp.where(here, grade_j, 0.0), axis=1, keepdims=True)
        length = jnp.broadcast_to(lengths[pl.ds(row, 1), :], (rows, 2 * rows))
        same = seg_j == seg_i
        live = slot_i < length
        allowed = (same & (slot_j <= slot_i) & live & (slot_j < length)) | (slot_i == slot_j)
        heads = sub // SUB == (lane // SUB) % HEADS
        mask[c] = jnp.where(allowed & heads, 1.0, 0.0)
        once = (lane // SUB) % HEADS == 0
        before = jnp.sum(jnp.where(once & (seg_j < seg_i), 1.0, 0.0), axis=1, keepdims=True)
        after = jnp.sum(
            jnp.where(once & same & (slot_j > slot_i), 1.0, 0.0), axis=1, keepdims=True
        )
        final = (after == 0.0) | (slot_i == length - 1)
        ends[c] = jnp.where(live & final, 1.0, 0.0)[:SUB, :1]
        levels[c] = grade_i[:SUB]
        position = slot_i[:SUB].astype(F32) - before[:SUB]
        lane = lane[:SUB]
        freqs = jnp.exp((lane % (HD // 2)).astype(F32) * (-2.0 * math.log(THETA) / HD))
        angles = position * freqs
        cosine[c] = jnp.cos(angles)
        sine[c] = jnp.where(lane < HD // 2, -1.0, 1.0) * jnp.sin(angles)
        return unused

    lax.fori_loop(0, chunks, make_tables, 0)

    @pl.when(section == 0)
    def _():
        load_x.wait()

    load_k.wait()
    load_v.wait()

    @pl.when((section > 0) & (section < last))
    def _():
        pl.semaphore_wait(barrier, 8)

    @pl.when((section == 0) | (section == last))
    def _():
        pl.semaphore_wait(barrier, 7)

    def turn(source, target):
        def block(t, unused):
            there = pl.ds(pl.multiple_of(t * 256, 256), 256)
            target[:, there] = source[there, :].T
            return unused

        lax.fori_loop(0, model // 256, block, 0)

    @pl.when(section > 0)
    def _():
        turn(wv, wvt)

    @pl.when(section > 1)
    def _():
        turn(wk, wkt)

    def columns(p):
        return pl.ds(p * piece, piece)

    def h_copy(c, p):
        return pltpu.make_async_remote_copy(
            src_ref=hout.at[c, :, columns(p)],
            dst_ref=hin.at[c, :, columns(p)],
            send_sem=hsend.at[c, p],
            recv_sem=hrecv.at[c, p],
            device_id={"section": up},
            device_id_type=MESH,
        )

    def g_copy(c, p):
        return pltpu.make_async_remote_copy(
            src_ref=gout.at[c, :, columns(p)],
            dst_ref=gin.at[c, :, columns(p)],
            send_sem=gsend.at[c, p],
            recv_sem=grecv.at[c, p],
            device_id={"section": down},
            device_id_type=MESH,
        )

    def x_copy(kind, c, r):
        peer = (x + r) % 4
        source, target = (
            (hin.at[c, :, pl.ds(pl.multiple_of(peer * piece, 128), piece)], peer_h),
            (mixs.at[c], peer_mix),
            (gin.at[c, :, pl.ds(pl.multiple_of(peer * piece, 128), piece)], peer_g),
            (gkv.at[c], peer_gkv),
        )[kind]
        return pltpu.make_async_remote_copy(
            src_ref=source,
            dst_ref=target.at[r - 1, c],
            send_sem=xsend.at[kind, c, r - 1],
            recv_sem=xrecv.at[kind, c, r - 1],
            device_id={"dp": xpeers[r - 1]},
            device_id_type=MESH,
        )

    def forward(c, n):
        some = pl.ds(c, n)
        lines = n * SUB
        row = c // 2

        def held(p):
            return hin[some, :, columns(p)].reshape(lines, piece)

        acc_k = jnp.zeros((lines, HEADS * HD), F32)
        acc_v = jnp.zeros((lines, HEADS * HD), F32)
        square = jnp.zeros((lines, 1), F32)
        for p in range(PIECES):

            @pl.when(section > 0)
            def _():
                for k in range(n):
                    h_copy(c + k, p).wait_recv()

            part = held(p)
            acc_k += dot(part, wk[columns(p), :])
            acc_v += dot(part, wv[columns(p), :])
            full = part.astype(F32)
            square += jnp.sum(full * full, axis=1, keepdims=True)
        scale = lax.rsqrt(square / model + EPS)
        scales[some] = scale.reshape(n, SUB, 1)
        turned = stack(acc_k * scale)
        turned = turned * tall(cosine[some]) + swap(turned) * tall(sine[some])
        key = turned.astype(BF16)
        value = stack(acc_v * scale).astype(BF16)
        keys[some] = key.reshape(n, rows, HD)
        values[some] = value.reshape(n, rows, HD)
        all_keys = keys[pl.ds(row * 2, 2)].reshape(2 * rows, HD)
        all_values = values[pl.ds(row * 2, 2)].reshape(2 * rows, HD)
        logits = dot_t(key, all_keys) * (1.0 / HD)
        logits = jnp.where(mask[some].reshape(n * rows, 2 * rows) > 0.0, logits, -1e30)
        top = jnp.max(logits, axis=1, keepdims=True)
        expd = jnp.exp(logits - top)
        prob = expd / jnp.sum(expd, axis=1, keepdims=True)
        probs[some] = prob.reshape(n, rows, 2 * rows)
        mixed = unstack(dot(prob.astype(BF16), all_values).astype(BF16))
        mixs[some] = mixed.reshape(n, SUB, HEADS * HD)

        def output(p, product):
            out = held(p).astype(F32) + product
            hout[some, :, columns(p)] = out.astype(BF16).reshape(n, SUB, piece)

        if n == 1:

            @pl.when(section == 0)
            def _():
                for p in range(PIECES):
                    output(p, dot_t(mixed, wv[columns(p), :]))
                    h_copy(c, p).start()

            @pl.when(section > 0)
            def _():
                for p in range(PIECES):
                    output(p, dot(mixed, wvt[:, columns(p)]))
                    h_copy(c, p).start()

        else:
            for p in range(PIECES):
                output(p, dot(mixed, wvt[:, columns(p)]))

        for k in range(n):
            for r in range(1, 4):
                x_copy(0, c + k, r).start()
                x_copy(1, c + k, r).start()

    def loss(c):
        some = pl.ds(c, 2)
        square = jnp.zeros((2, SUB, 1), F32)
        score = jnp.zeros((2, SUB, 1), F32)
        for p in range(PIECES):
            full = hout[some, :, columns(p)].astype(F32)
            square += jnp.sum(full * full, axis=2, keepdims=True)
            score += jnp.sum(full * wscore[:, columns(p)][None], axis=2, keepdims=True)
        scale = lax.rsqrt(square / model + EPS)
        score = score * scale
        end = ends[some]

        def softmax(entries):
            masked = jnp.where(end > 0.0, entries, -1e30)
            top = jnp.max(jnp.max(masked, axis=0), axis=0, keepdims=True)
            expd = jnp.where(end > 0.0, jnp.exp(masked - top[None]), 0.0)
            return expd / jnp.sum(jnp.sum(expd, axis=0), axis=0, keepdims=True)[None]

        weight = jnp.where(end > 0.0, softmax(score) - softmax(levels[some]), 0.0)
        first = scale * weight
        second = scale * scale * weight * score * (1.0 / model)
        for p in range(PIECES):
            full = hout[some, :, columns(p)].astype(F32)
            grad = first * wscore[:, columns(p)][None] - second * full
            gin[some, :, columns(p)] = grad.astype(BF16)

    def backward(c, n):
        some = pl.ds(c, n)
        lines = n * SUB
        row = c // 2

        def grad_at(p):
            return gin[some, :, columns(p)].reshape(lines, piece)

        acc = jnp.zeros((lines, HEADS * HD), F32)
        for p in range(PIECES):
            if n == 1:
                g_copy(c, p).wait_recv()
            acc += dot(grad_at(p), wv[columns(p), :])
        scale = scales[some].reshape(lines, 1)
        grad_mixed = stack(acc).astype(BF16)
        all_keys = keys[pl.ds(row * 2, 2)].reshape(2 * rows, HD)
        all_values = values[pl.ds(row * 2, 2)].reshape(2 * rows, HD)
        key = keys[some].reshape(n * rows, HD)
        value = values[some].reshape(n * rows, HD)
        prob = probs[some].reshape(n * rows, 2 * rows)
        grad_probs = dot_t(grad_mixed, all_values)
        product = prob * grad_probs
        grad_scores = (product - prob * jnp.sum(product, axis=1, keepdims=True)).astype(BF16)
        own_v = t_dot(prob.astype(BF16), grad_mixed)
        own_k = t_dot(grad_scores, key)
        if n == 1:
            second = lax.rem(c, 2) == 1
            from_v, from_k = own_v, own_k
            own_v = jnp.where(second, from_v[rows:], from_v[:rows] + carry_v[...])
            own_k = jnp.where(second, from_k[rows:], from_k[:rows] + carry_k[...])
            carry_v[...] = from_v[:rows]
            carry_k[...] = from_k[:rows]
        turned = (dot(grad_scores, all_keys) + own_k) * (1.0 / HD)
        along = jnp.sum(turned * key.astype(F32) + own_v * value.astype(F32), axis=1, keepdims=True)
        along = jnp.sum(along.reshape(n, HEADS, SUB, 1), axis=1).reshape(lines, 1)
        along = along * (scale * scale) * (1.0 / model)
        grad_key = turned * tall(cosine[some]) - swap(turned) * tall(sine[some])
        flat_key = unstack(grad_key.astype(BF16))
        flat_value = unstack(own_v.astype(BF16))
        features = HEADS * HD
        key_part = (flat_key.astype(F32) * scale).astype(BF16)
        value_part = (flat_value.astype(F32) * scale).astype(BF16)
        gkv[some, :, :features] = key_part.reshape(n, SUB, features)
        gkv[some, :, features:] = value_part.reshape(n, SUB, features)

        @pl.when(section > 0)
        def _():
            for p in range(PIECES):
                grad = dot(flat_key, wkt[:, columns(p)]) + dot(flat_value, wvt[:, columns(p)])
                full = hin[some, :, columns(p)].reshape(lines, piece).astype(F32)
                out = grad_at(p).astype(F32) + scale * grad - along * full
                gout[some, :, columns(p)] = out.astype(BF16).reshape(n, SUB, piece)
                g_copy(c + n - 1, p).start()
            if n == 2:
                for p in range(PIECES):
                    g_copy(c, p).start()

        for k in range(n):
            for r in range(1, 4):
                x_copy(2, c + k, r).start()
                x_copy(3, c + k, r).start()

    tile = 256
    group = chunks // 2

    def weights(base):
        def arrive(c, unused):
            for kind in range(4):
                for r in range(1, 4):
                    x_copy(kind, base + c, r).wait_recv()
            return unused

        lax.fori_loop(0, group, arrive, 0)
        which = pl.ds(base, group)

        def gather(own, peers):
            own = own.reshape(group * SUB, own.shape[-1])
            peers = peers.reshape(3 * group * SUB, peers.shape[-1])
            return jnp.concatenate([own, peers], axis=0)

        def block(t, unused):
            there = pl.ds(pl.multiple_of(t * tile, tile), tile)
            mine = pl.ds(pl.multiple_of(x * piece + t * tile, 128), tile)
            hidden = gather(hin[which, :, mine], peer_h[:, which, :, there])
            grads = gather(gin[which, :, mine], peer_g[:, which, :, there])
            both = gather(gkv[which], peer_gkv[:, which])
            mixed = gather(mixs[which], peer_mix[:, which])
            features = HEADS * HD
            part_key = t_dot(hidden, both[:, :features])
            part_value = t_dot(hidden, both[:, features:]) + t_dot(grads, mixed)

            @pl.when(base == 0)
            def _():
                total[there, :features] = part_key
                total[there, features:] = part_value

            @pl.when(base > 0)
            def _():
                total[there, :features] = part_key + total[there, :features]
                total[there, features:] = part_value + total[there, features:]

            return unused

        lax.fori_loop(0, piece // tile, block, 0)

    share = piece // 8
    half_features = HEADS * HD
    sides = [pl.ds(0, half_features), pl.ds(half_features, half_features)]

    def rows_of(ypart, corepart):
        return pl.ds(pl.multiple_of((ypart * 2 + corepart) * share, 32), share)

    def pair_copy(k):
        return pltpu.make_async_remote_copy(
            src_ref=pair_out.at[k],
            dst_ref=pair_in.at[k],
            send_sem=pair_send.at[k],
            recv_sem=pair_recv.at[k],
            device_id={"dp": sibling},
            device_id_type=MESH,
        )

    def first_copy(side, k):
        return pltpu.make_async_remote_copy(
            src_ref=first_out.at[side, k],
            dst_ref=first_in.at[side, k],
            send_sem=first_send.at[side, k],
            recv_sem=first_recv.at[side, k],
            device_id={"dp": ydevices[side]},
            device_id_type=MESH,
        )

    def second_copy(side):
        return pltpu.make_async_remote_copy(
            src_ref=second_out.at[side],
            dst_ref=second_in.at[side],
            send_sem=second_send.at[side],
            recv_sem=second_recv.at[side],
            device_id={"dp": ydevices[1 - side]},
            device_id_type=MESH,
        )

    def scatter():
        order = [opposite, beside, across, y]
        for k in range(4):
            pair_out[k] = total[rows_of(order[k], 1 - core), :].astype(BF16)
            pair_copy(k).start()

        def held(k, side):
            return total[rows_of(order[k], core), sides[side]] + pair_in[k, :, sides[side]].astype(F32)

        pair_copy(0).wait_recv()
        for side in range(2):
            first_out[side, 1] = held(0, side).astype(BF16)
            first_copy(side, 1).start()
        for side in range(2):
            pair_copy(1 + side).wait_recv()
            first_out[side, 0] = held(1 + side, side).astype(BF16)
            first_copy(side, 0).start()
        for side in range(2):
            first_copy(side, 1).wait_recv()
            second_out[side] = (held(2 - side, side) + first_in[side, 1].astype(F32)).astype(BF16)
            second_copy(side).start()
        pair_copy(3).wait_recv()
        for side, out in ((0, out_key), (1, out_value)):
            first_copy(side, 0).wait_recv()
            second_copy(side).wait_recv()
            out[...] = held(3, side) + first_in[side, 0].astype(F32) + second_in[side].astype(F32)
        for k in range(4):
            pair_copy(k).wait_send()
        for side in range(2):
            first_copy(side, 0).wait_send()
            first_copy(side, 1).wait_send()
            second_copy(side).wait_send()

    lead = jnp.where(section == last - 1, 5, chunks)

    def slot(i, unused):
        @pl.when(i < chunks)
        def _():
            forward(i, 1)

        j = i - lead

        @pl.when((j == 0) & (section == 1))
        def _():
            turn(wk, wkt)

        @pl.when((j >= 0) & (j < chunks))
        def _():
            backward((j // 2) * 2 + 1 - lax.rem(j, 2), 1)

        @pl.when(j == group + 1)
        def _():
            weights(0)

        return unused

    def whole(row, unused):
        forward(row * 2, 2)
        loss(row * 2)
        backward(row * 2, 2)
        return unused

    @pl.when(section < last)
    def _():
        lax.fori_loop(0, 2 * chunks, slot, 0)

    @pl.when(section == last)
    def _():
        lax.fori_loop(0, chunks // 2, whole, 0)

    def rest(step, unused):
        weights(step * group)
        return unused

    lax.fori_loop(jnp.where(section == last, 0, 1), 2, rest, 0)
    scatter()

    def drain(c, unused):
        for p in range(PIECES):

            @pl.when(section < last)
            def _():
                h_copy(c, p).wait_send()

            @pl.when(section > 0)
            def _():
                g_copy(c, p).wait_send()

        for kind in range(4):
            for r in range(1, 4):
                x_copy(kind, c, r).wait_send()
        return unused

    lax.fori_loop(0, chunks, drain, 0)


def shards(x0, w_key, w_value, w_score, segments, lengths, grades):
    sections = lax.axis_size("section")
    micro, width, model = x0.shape
    features = w_key.shape[2]
    chunks = micro * width // SUB
    vmem = pl.BlockSpec(memory_space=pltpu.VMEM)
    act = (chunks, SUB, model)
    flat = (chunks, SUB, features)
    stacked = (chunks, HEADS * SUB, HD)
    piece = model // PIECES
    share = piece // 8
    dma = pltpu.SemaphoreType.DMA
    grad_key, grad_value = pl.pallas_call(
        functools.partial(pipe_kernel, sections),
        out_shape=[jax.ShapeDtypeStruct((share, features), F32)] * 2,
        in_specs=[pl.BlockSpec(memory_space=pl.ANY)] * 3 + [vmem] * 4,
        out_specs=[vmem] * 2,
        scratch_shapes=[
            pltpu.VMEM((model, features), BF16),
            pltpu.VMEM((model, features), BF16),
            pltpu.VMEM((features, model), BF16),
            pltpu.VMEM((features, model), BF16),
            pltpu.VMEM((2 * micro, HD), F32),
            pltpu.VMEM((chunks, SUB, HD), F32),
            pltpu.VMEM((chunks, SUB, HD), F32),
            pltpu.VMEM((chunks, HEADS * SUB, 2 * HEADS * SUB), F32),
            pltpu.VMEM((chunks, SUB, 1), F32),
            pltpu.VMEM((chunks, SUB, 1), F32),
            pltpu.VMEM(act, BF16),
            pltpu.VMEM(act, BF16),
            pltpu.VMEM((chunks, SUB, 2 * features), BF16),
            pltpu.VMEM(flat, BF16),
            pltpu.VMEM(act, BF16),
            pltpu.VMEM(act, BF16),
            pltpu.VMEM(stacked, BF16),
            pltpu.VMEM(stacked, BF16),
            pltpu.VMEM((chunks, HEADS * SUB, 2 * HEADS * SUB), F32),
            pltpu.VMEM((chunks, SUB, 1), F32),
            pltpu.VMEM((HEADS * SUB, HD), F32),
            pltpu.VMEM((HEADS * SUB, HD), F32),
            pltpu.VMEM((3, chunks, SUB, piece), BF16),
            pltpu.VMEM((3, chunks, SUB, piece), BF16),
            pltpu.VMEM((3, chunks, SUB, 2 * features), BF16),
            pltpu.VMEM((3, chunks, SUB, features), BF16),
            pltpu.VMEM((piece, 2 * features), F32),
            pltpu.VMEM((4, share, 2 * features), BF16),
            pltpu.VMEM((4, share, 2 * features), BF16),
            pltpu.VMEM((2, 2, share, features), BF16),
            pltpu.VMEM((2, 2, share, features), BF16),
            pltpu.VMEM((2, share, features), BF16),
            pltpu.VMEM((2, share, features), BF16),
            dma,
            dma((2,)),
            dma((chunks, PIECES)),
            dma((chunks, PIECES)),
            dma((chunks, PIECES)),
            dma((chunks, PIECES)),
            dma((4, chunks, 3)),
            dma((4, chunks, 3)),
            dma((4,)),
            dma((4,)),
            dma((2, 2)),
            dma((2, 2)),
            dma((2,)),
            dma((2,)),
        ],
        compiler_params=pltpu.CompilerParams(
            collective_id=0, has_side_effects=True, vmem_limit_bytes=56 * 2**20
        ),
    )(
        x0.reshape(act),
        w_key[0],
        w_value[0],
        w_score.reshape(1, model),
        segments,
        lengths,
        grades,
    )
    return (grad_key[None], grad_value[None])


def solution(mesh):
    placed = (
        P(None, "dp", None),
        P("section", None, None),
        P("section", None, None),
        P(),
        P(None, "dp"),
        P(None, "dp"),
        P(None, "dp"),
    )
    return jax.shard_map(
        shards,
        mesh=mesh,
        in_specs=placed,
        out_specs=(P("section", "dp", None), P("section", "dp", None)),
        check_vma=False,
    )
```

time: 225 us -> 177 us (0.79)
  Pallas kernels: 209 us -> 171 us
  other arithmetic: 7.15 us -> 0 us
  local copies, waits for them, and re-layouts: 7.24 us -> 4.75 us
    pallas_call x1, Pallas kernels: 209 us -> 171 us  [shards(): pl.pallas_call(functools.partial(pipe_kernel, sections), out_shape=[jax.S...]
    unnamed x2 -> x3, local copies, waits for them, and re-layouts: 3.44 us -> 4.75 us
where the time goes in v3:
time: 177 us
  Pallas kernels  171 us (97%)
  local copies, waits for them, and re-layouts  4.75 us (3%)
    pallas_call x1, Pallas kernels, shards(): pl.pallas_call(functools.partial(pipe_kernel, sections), out_shape=[jax.S...  171 us
    unnamed x3, local copies, waits for them, and re-layouts  4.75 us

profile of v3, /device:TPU:1, one launch (start us, length us, event | category | flops | bytes accessed | tf_op | source)
XLA Modules:
  0.0 176.6 jit_solution(2835492763026981225)
XLA Ops:
  0.6 1.3 copy.9.lengths
  1.9 171.3 %shard_map.86 = (f32[160,512]{1,0:T(8,128)}, f32[160,512]{1,0:T(8,128)}) custom-call(bf16[8,16,5120]{2,1,0:T(8,128)(2,1)} %bitcast.8, bf16[5120,512]{1,0:T(8,128)(2,1)} %bitcast.6, bf16[5120,512]{1,0:T(8,128)(2,1)} %bitcast.7, f32[1,5120]{1,0:T(1,128)} %bitcast.11, s32[4,32]{1,0:T(4,128)} %segments.1, s32[4,1]{1,0:T(4,128)} %copy.9.lengths, s32[4,32]{1,0:T(4,128)} %grades.1), custom_call_target="tpu_custom_call" | custom-call | tf_op jit(solution)/shard_map/pallas_call | solution.py:615
  173.2 1.7 copy.12
  174.9 1.7 copy.13

commit v4 on v3

--- a/solution.py
+++ b/solution.py
@@ -14,6 +14,7 @@
 THETA = 1000000.0
 SUB = 16
 PIECES = 4
+STRIPS = 5
 MESH = pl.DeviceIdType.MESH
 F32 = jnp.float32
 BF16 = jnp.bfloat16
@@ -98,7 +99,6 @@
     first_in,
     second_out,
     second_in,
-    local_sem,
     weight_sem,
     hsend,
     hrecv,
@@ -126,19 +126,27 @@
     chunks = hin.shape[0]
     model = hin.shape[2]
     piece = model // PIECES
+    strip = model // STRIPS
     up = jnp.minimum(section + 1, last)
     down = jnp.maximum(section - 1, 0)
 
     rows = HEADS * SUB
     load_k = pltpu.make_async_copy(wk_all, wk, weight_sem.at[0])
     load_v = pltpu.make_async_copy(wv_all, wv, weight_sem.at[1])
-    load_x = pltpu.make_async_copy(x0, hin, local_sem)
     load_k.start()
     load_v.start()
 
     @pl.when(section == 0)
     def _():
-        load_x.start()
+        def load(c, unused):
+            for p in range(STRIPS):
+                there = pl.ds(p * strip, strip)
+                pltpu.make_async_copy(
+                    x0.at[c, :, there], hin.at[c, :, there], hrecv.at[c, p]
+                ).start()
+            return unused
+
+        lax.fori_loop(0, chunks, load, 0)
 
     barrier = pltpu.get_barrier_semaphore()
 
@@ -172,7 +180,11 @@
         here = lane == half * rows + sub
         seg_i = jnp.sum(jnp.where(here, seg_j, 0.0), axis=1, keepdims=True)
         grade_i = jnp.sum(jnp.where(here, grade_j, 0.0), axis=1, keepdims=True)
-        length = jnp.broadcast_to(lengths[pl.ds(row, 1), :], (rows, 2 * rows))
+        entry = lax.broadcasted_iota(jnp.int32, lengths.shape, 1)
+        length = jnp.sum(
+            jnp.where(entry == row, lengths[...].astype(F32), 0.0), axis=1, keepdims=True
+        )
+        length = jnp.broadcast_to(length, (rows, 2 * rows)).astype(jnp.int32)
         same = seg_j == seg_i
         live = slot_i < length
         allowed = (same & (slot_j <= slot_i) & live & (slot_j < length)) | (slot_i == slot_j)
@@ -196,10 +208,6 @@
 
     lax.fori_loop(0, chunks, make_tables, 0)
 
-    @pl.when(section == 0)
-    def _():
-        load_x.wait()
-
     load_k.wait()
     load_v.wait()
 
@@ -228,7 +236,7 @@
         turn(wk, wkt)
 
     def columns(p):
-        return pl.ds(p * piece, piece)
+        return pl.ds(p * strip, strip)
 
     def h_copy(c, p):
         return pltpu.make_async_remote_copy(
@@ -273,18 +281,14 @@
         row = c // 2
 
         def held(p):
-            return hin[some, :, columns(p)].reshape(lines, piece)
+            return hin[some, :, columns(p)].reshape(lines, strip)
 
         acc_k = jnp.zeros((lines, HEADS * HD), F32)
         acc_v = jnp.zeros((lines, HEADS * HD), F32)
         square = jnp.zeros((lines, 1), F32)
-        for p in range(PIECES):
-
-            @pl.when(section > 0)
-            def _():
-                for k in range(n):
-                    h_copy(c + k, p).wait_recv()
-
+        for p in range(STRIPS):
+            for k in range(n):
+                h_copy(c + k, p).wait_recv()
             part = held(p)
             acc_k += dot(part, wk[columns(p), :])
             acc_v += dot(part, wv[columns(p), :])
@@ -311,24 +315,24 @@
 
         def output(p, product):
             out = held(p).astype(F32) + product
-            hout[some, :, columns(p)] = out.astype(BF16).reshape(n, SUB, piece)
+            hout[some, :, columns(p)] = out.astype(BF16).reshape(n, SUB, strip)
 
         if n == 1:
 
             @pl.when(section == 0)
             def _():
-                for p in range(PIECES):
+                for p in range(STRIPS):
                     output(p, dot_t(mixed, wv[columns(p), :]))
                     h_copy(c, p).start()
 
             @pl.when(section > 0)
             def _():
-                for p in range(PIECES):
+                for p in range(STRIPS):
                     output(p, dot(mixed, wvt[:, columns(p)]))
                     h_copy(c, p).start()
 
         else:
-            for p in range(PIECES):
+            for p in range(STRIPS):
                 output(p, dot(mixed, wvt[:, columns(p)]))
 
         for k in range(n):
@@ -340,7 +344,7 @@
         some = pl.ds(c, 2)
         square = jnp.zeros((2, SUB, 1), F32)
         score = jnp.zeros((2, SUB, 1), F32)
-        for p in range(PIECES):
+        for p in range(STRIPS):
             full = hout[some, :, columns(p)].astype(F32)
             square += jnp.sum(full * full, axis=2, keepdims=True)
             score += jnp.sum(full * wscore[:, columns(p)][None], axis=2, keepdims=True)
@@ -357,7 +361,7 @@
         weight = jnp.where(end > 0.0, softmax(score) - softmax(levels[some]), 0.0)
         first = scale * weight
         second = scale * scale * weight * score * (1.0 / model)
-        for p in range(PIECES):
+        for p in range(STRIPS):
             full = hout[some, :, columns(p)].astype(F32)
             grad = first * wscore[:, columns(p)][None] - second * full
             gin[some, :, columns(p)] = grad.astype(BF16)
@@ -368,10 +372,10 @@
         row = c // 2
 
         def grad_at(p):
-            return gin[some, :, columns(p)].reshape(lines, piece)
+            return gin[some, :, columns(p)].reshape(lines, strip)
 
         acc = jnp.zeros((lines, HEADS * HD), F32)
-        for p in range(PIECES):
+        for p in range(STRIPS):
             if n == 1:
                 g_copy(c, p).wait_recv()
             acc += dot(grad_at(p), wv[columns(p), :])
@@ -409,14 +413,14 @@
 
         @pl.when(section > 0)
         def _():
-            for p in range(PIECES):
+            for p in range(STRIPS):
                 grad = dot(flat_key, wkt[:, columns(p)]) + dot(flat_value, wvt[:, columns(p)])
-                full = hin[some, :, columns(p)].reshape(lines, piece).astype(F32)
+                full = hin[some, :, columns(p)].reshape(lines, strip).astype(F32)
                 out = grad_at(p).astype(F32) + scale * grad - along * full
-                gout[some, :, columns(p)] = out.astype(BF16).reshape(n, SUB, piece)
+                gout[some, :, columns(p)] = out.astype(BF16).reshape(n, SUB, strip)
                 g_copy(c + n - 1, p).start()
             if n == 2:
-                for p in range(PIECES):
+                for p in range(STRIPS):
                     g_copy(c, p).start()
 
         for k in range(n):
@@ -554,7 +558,7 @@
         def _():
             backward((j // 2) * 2 + 1 - lax.rem(j, 2), 1)
 
-        @pl.when(j == group + 1)
+        @pl.when((j == group + 1) & (section == 0))
         def _():
             weights(0)
 
@@ -578,11 +582,11 @@
         weights(step * group)
         return unused
 
-    lax.fori_loop(jnp.where(section == last, 0, 1), 2, rest, 0)
+    lax.fori_loop(jnp.where(section == 0, 1, 0), 2, rest, 0)
     scatter()
 
     def drain(c, unused):
-        for p in range(PIECES):
+        for p in range(STRIPS):
 
             @pl.when(section < last)
             def _():
@@ -598,6 +602,11 @@
         return unused
 
     lax.fori_loop(0, chunks, drain, 0)
+
+
+def finish_kernel(key_in, value_in, key_out, value_out):
+    key_out[0] = key_in[...]
+    value_out[0] = value_in[...]
 
 
 def shards(x0, w_key, w_value, w_score, segments, lengths, grades):
@@ -651,12 +660,11 @@
             pltpu.VMEM((2, 2, share, features), BF16),
             pltpu.VMEM((2, share, features), BF16),
             pltpu.VMEM((2, share, features), BF16),
-            dma,
             dma((2,)),
-            dma((chunks, PIECES)),
-            dma((chunks, PIECES)),
-            dma((chunks, PIECES)),
-            dma((chunks, PIECES)),
+            dma((chunks, STRIPS)),
+            dma((chunks, STRIPS)),
+            dma((chunks, STRIPS)),
+            dma((chunks, STRIPS)),
             dma((4, chunks, 3)),
             dma((4, chunks, 3)),
             dma((4,)),
@@ -675,10 +683,16 @@
         w_value[0],
         w_score.reshape(1, model),
         segments,
-        lengths,
+        lengths.reshape(1, micro),
         grades,
     )
-    return (grad_key[None], grad_value[None])
+    grad_key, grad_value = pl.pallas_call(
+        finish_kernel,
+        out_shape=[jax.ShapeDtypeStruct((1, share, features), F32)] * 2,
+        in_specs=[vmem] * 2,
+        out_specs=[vmem] * 2,
+    )(grad_key, grad_value)
+    return (grad_key, grad_value)
 
 
 def solution(mesh):

time: 177 us -> 168 us (0.949)
  local copies, waits for them, and re-layouts: 4.75 us -> 0 us
  Pallas kernels: 171 us -> 167 us
    pallas_call x1, Pallas kernels: 171 us -> 165 us  [shards(): pl.pallas_call(functools.partial(pipe_kernel, sections), out_shape=[jax.S...]
    unnamed x3 -> x0, local copies, waits for them, and re-layouts: 4.75 us -> none
    pallas_call x0 -> x1, Pallas kernels: none -> 1.93 us  [shards(): pl.pallas_call(finish_kernel, out_shape=[jax.ShapeDtypeStruct((1, share,...]
where the time goes in v4:
time: 168 us
  Pallas kernels  167 us (99%)
    pallas_call x1, Pallas kernels, shards(): pl.pallas_call(functools.partial(pipe_kernel, sections), out_shape=[jax.S...  165 us

profile of v4, /device:TPU:1, one launch (start us, length us, event | category | flops | bytes accessed | tf_op | source)
XLA Modules:
  0.0 167.7 jit_solution(11059597410460443586)
XLA Ops:
  0.6 165.2 %shard_map.86 = (f32[160,512]{1,0:T(8,128)}, f32[160,512]{1,0:T(8,128)}) custom-call(bf16[8,16,5120]{2,1,0:T(8,128)(2,1)} %bitcast.7, bf16[5120,512]{1,0:T(8,128)(2,1)} %bitcast.5, bf16[5120,512]{1,0:T(8,128)(2,1)} %bitcast.6, f32[1,5120]{1,0:T(1,128)} %bitcast.8, s32[4,32]{1,0:T(4,128)} %segments.1, s32[1,4]{1,0:T(1,128)} %bitcast.9, s32[4,32]{1,0:T(4,128)} %grades.1), custom_call_target="tpu_custom_call" | custom-call | tf_op jit(solution)/shard_map/pallas_call | solution.py:624
  165.8 1.9 %shard_map.87 = (f32[1,160,512]{2,1,0:T(8,128)}, f32[1,160,512]{2,1,0:T(8,128)}) custom-call(f32[160,512]{1,0:T(8,128)} %get-tuple-element.4.key_in, f32[160,512]{1,0:T(8,128)} %get-tuple-element.5.value_in), custom_call_target="tpu_custom_call" | custom-call | tf_op jit(solution)/shard_map/pallas_call | solution.py:689

commit v5 on v4

--- a/solution.py
+++ b/solution.py
@@ -14,7 +14,8 @@
 THETA = 1000000.0
 SUB = 16
 PIECES = 4
-STRIPS = 5
+BOUNDS = (0, 1024, 2048, 3072, 4096, 5120)
+STRIPS = len(BOUNDS) - 1
 MESH = pl.DeviceIdType.MESH
 F32 = jnp.float32
 BF16 = jnp.bfloat16
@@ -53,6 +54,16 @@
 
 def tall(array):
     return jnp.concatenate([array[k] for k in range(array.shape[0]) for h in range(HEADS)], axis=0)
+
+
+def ahead(compute, finish):
+    finish(0, compute(0))
+    waiting = compute(1)
+    for p in range(2, STRIPS):
+        following = compute(p)
+        finish(p - 1, waiting)
+        waiting = following
+    finish(STRIPS - 1, waiting)
 
 
 def pipe_kernel(
@@ -126,21 +137,29 @@
     chunks = hin.shape[0]
     model = hin.shape[2]
     piece = model // PIECES
-    strip = model // STRIPS
     up = jnp.minimum(section + 1, last)
     down = jnp.maximum(section - 1, 0)
 
+    def columns(p):
+        return pl.ds(BOUNDS[p], BOUNDS[p + 1] - BOUNDS[p])
+
     rows = HEADS * SUB
-    load_k = pltpu.make_async_copy(wk_all, wk, weight_sem.at[0])
-    load_v = pltpu.make_async_copy(wv_all, wv, weight_sem.at[1])
-    load_k.start()
-    load_v.start()
+    def load_weight(p):
+        there = columns(p)
+        return [
+            pltpu.make_async_copy(source.at[there], target.at[there], weight_sem.at[k, p])
+            for k, source, target in ((0, wk_all, wk), (1, wv_all, wv))
+        ]
+
+    for p in range(STRIPS):
+        for copy in load_weight(p):
+            copy.start()
 
     @pl.when(section == 0)
     def _():
         def load(c, unused):
             for p in range(STRIPS):
-                there = pl.ds(p * strip, strip)
+                there = columns(p)
                 pltpu.make_async_copy(
                     x0.at[c, :, there], hin.at[c, :, there], hrecv.at[c, p]
                 ).start()
@@ -208,8 +227,11 @@
 
     lax.fori_loop(0, chunks, make_tables, 0)
 
-    load_k.wait()
-    load_v.wait()
+    @pl.when(section > 0)
+    def _():
+        for p in range(STRIPS):
+            for copy in load_weight(p):
+                copy.wait()
 
     @pl.when((section > 0) & (section < last))
     def _():
@@ -234,9 +256,6 @@
     @pl.when(section > 1)
     def _():
         turn(wk, wkt)
-
-    def columns(p):
-        return pl.ds(p * strip, strip)
 
     def h_copy(c, p):
         return pltpu.make_async_remote_copy(
@@ -281,7 +300,8 @@
         row = c // 2
 
         def held(p):
-            return hin[some, :, columns(p)].reshape(lines, strip)
+            part = hin[some, :, columns(p)]
+            return part.reshape(lines, part.shape[-1])
 
         acc_k = jnp.zeros((lines, HEADS * HD), F32)
         acc_v = jnp.zeros((lines, HEADS * HD), F32)
@@ -289,6 +309,13 @@
         for p in range(STRIPS):
             for k in range(n):
                 h_copy(c + k, p).wait_recv()
+            if n == 1:
+
+                @pl.when((section == 0) & (c == 0))
+                def _():
+                    for copy in load_weight(p):
+                        copy.wait()
+
             part = held(p)
             acc_k += dot(part, wk[columns(p), :])
             acc_v += dot(part, wv[columns(p), :])
@@ -313,27 +340,26 @@
         mixed = unstack(dot(prob.astype(BF16), all_values).astype(BF16))
         mixs[some] = mixed.reshape(n, SUB, HEADS * HD)
 
-        def output(p, product):
-            out = held(p).astype(F32) + product
-            hout[some, :, columns(p)] = out.astype(BF16).reshape(n, SUB, strip)
+        def strip_of(p, product):
+            return (held(p).astype(F32) + product).astype(BF16).reshape(n, SUB, -1)
+
+        def send(p, out):
+            hout[some, :, columns(p)] = out
+            if n == 1:
+                h_copy(c, p).start()
 
         if n == 1:
 
             @pl.when(section == 0)
             def _():
-                for p in range(STRIPS):
-                    output(p, dot_t(mixed, wv[columns(p), :]))
-                    h_copy(c, p).start()
+                ahead(lambda p: strip_of(p, dot_t(mixed, wv[columns(p), :])), send)
 
             @pl.when(section > 0)
             def _():
-                for p in range(STRIPS):
-                    output(p, dot(mixed, wvt[:, columns(p)]))
-                    h_copy(c, p).start()
+                ahead(lambda p: strip_of(p, dot(mixed, wvt[:, columns(p)])), send)
 
         else:
-            for p in range(STRIPS):
-                output(p, dot(mixed, wvt[:, columns(p)]))
+            ahead(lambda p: strip_of(p, dot(mixed, wvt[:, columns(p)])), send)
 
         for k in range(n):
             for r in range(1, 4):
@@ -372,7 +398,8 @@
         row = c // 2
 
         def grad_at(p):
-            return gin[some, :, columns(p)].reshape(lines, strip)
+            part = gin[some, :, columns(p)]
+            return part.reshape(lines, part.shape[-1])
 
         acc = jnp.zeros((lines, HEADS * HD), F32)
         for p in range(STRIPS):
@@ -413,12 +440,17 @@
 
         @pl.when(section > 0)
         def _():
-            for p in range(STRIPS):
+            def strip_of(p):
                 grad = dot(flat_key, wkt[:, columns(p)]) + dot(flat_value, wvt[:, columns(p)])
-                full = hin[some, :, columns(p)].reshape(lines, strip).astype(F32)
+                full = hin[some, :, columns(p)].reshape(lines, -1).astype(F32)
                 out = grad_at(p).astype(F32) + scale * grad - along * full
-                gout[some, :, columns(p)] = out.astype(BF16).reshape(n, SUB, strip)
+                return out.astype(BF16).reshape(n, SUB, -1)
+
+            def send(p, out):
+                gout[some, :, columns(p)] = out
                 g_copy(c + n - 1, p).start()
+
+            ahead(strip_of, send)
             if n == 2:
                 for p in range(STRIPS):
                     g_copy(c, p).start()
@@ -430,6 +462,23 @@
 
     tile = 256
     group = chunks // 2
+
+    share = piece // 8
+    half_features = HEADS * HD
+    sides = [pl.ds(0, half_features), pl.ds(half_features, half_features)]
+
+    def rows_of(ypart, corepart):
+        return pl.ds(pl.multiple_of((ypart * 2 + corepart) * share, 32), share)
+
+    def pair_copy(k):
+        return pltpu.make_async_remote_copy(
+            src_ref=pair_out.at[k],
+            dst_ref=pair_in.at[k],
+            send_sem=pair_send.at[k],
+            recv_sem=pair_recv.at[k],
+            device_id={"dp": sibling},
+            device_id_type=MESH,
+        )
 
     def weights(base):
         def arrive(c, unused):
@@ -467,26 +516,17 @@
                 total[there, :features] = part_key + total[there, :features]
                 total[there, features:] = part_value + total[there, features:]
 
+            for k in range(4):
+                ready = ((k * 2 + 2 - core) * share + tile - 1) // tile - 1
+
+                @pl.when((base > 0) & (t == ready))
+                def _():
+                    pair_out[k] = total[rows_of(k, 1 - core), :].astype(BF16)
+                    pair_copy(k).start()
+
             return unused
 
         lax.fori_loop(0, piece // tile, block, 0)
-
-    share = piece // 8
-    half_features = HEADS * HD
-    sides = [pl.ds(0, half_features), pl.ds(half_features, half_features)]
-
-    def rows_of(ypart, corepart):
-        return pl.ds(pl.multiple_of((ypart * 2 + corepart) * share, 32), share)
-
-    def pair_copy(k):
-        return pltpu.make_async_remote_copy(
-            src_ref=pair_out.at[k],
-            dst_ref=pair_in.at[k],
-            send_sem=pair_send.at[k],
-            recv_sem=pair_recv.at[k],
-            device_id={"dp": sibling},
-            device_id_type=MESH,
-        )
 
     def first_copy(side, k):
         return pltpu.make_async_remote_copy(
@@ -511,25 +551,22 @@
     def scatter():
         order = [opposite, beside, across, y]
         for k in range(4):
-            pair_out[k] = total[rows_of(order[k], 1 - core), :].astype(BF16)
-            pair_copy(k).start()
+            pair_copy(k).wait_recv()
 
         def held(k, side):
-            return total[rows_of(order[k], core), sides[side]] + pair_in[k, :, sides[side]].astype(F32)
-
-        pair_copy(0).wait_recv()
+            other = pair_in[order[k], :, sides[side]].astype(F32)
+            return total[rows_of(order[k], core), sides[side]] + other
+
         for side in range(2):
             first_out[side, 1] = held(0, side).astype(BF16)
             first_copy(side, 1).start()
         for side in range(2):
-            pair_copy(1 + side).wait_recv()
             first_out[side, 0] = held(1 + side, side).astype(BF16)
             first_copy(side, 0).start()
         for side in range(2):
             first_copy(side, 1).wait_recv()
             second_out[side] = (held(2 - side, side) + first_in[side, 1].astype(F32)).astype(BF16)
             second_copy(side).start()
-        pair_copy(3).wait_recv()
         for side, out in ((0, out_key), (1, out_value)):
             first_copy(side, 0).wait_recv()
             second_copy(side).wait_recv()
@@ -660,7 +697,7 @@
             pltpu.VMEM((2, 2, share, features), BF16),
             pltpu.VMEM((2, share, features), BF16),
             pltpu.VMEM((2, share, features), BF16),
-            dma((2,)),
+            dma((2, STRIPS)),
             dma((chunks, STRIPS)),
             dma((chunks, STRIPS)),
             dma((chunks, STRIPS)),

time: 168 us -> 165 us (0.982)
  Pallas kernels: 167 us -> 164 us
    pallas_call x1, Pallas kernels: 165 us -> 163 us  [shards(): pl.pallas_call(functools.partial(pipe_kernel, sections), out_shape=[jax.S...]
where the time goes in v5:
time: 165 us
  Pallas kernels  164 us (99%)
    pallas_call x1, Pallas kernels, shards(): pl.pallas_call(functools.partial(pipe_kernel, sections), out_shape=[jax.S...  163 us

profile of v5, /device:TPU:1, one launch (start us, length us, event | category | flops | bytes accessed | tf_op | source)
XLA Modules:
  0.0 165.1 jit_solution(7621804000367079797)
XLA Ops:
  0.6 162.6 %shard_map.86 = (f32[160,512]{1,0:T(8,128)}, f32[160,512]{1,0:T(8,128)}) custom-call(bf16[8,16,5120]{2,1,0:T(8,128)(2,1)} %bitcast.7, bf16[5120,512]{1,0:T(8,128)(2,1)} %bitcast.5, bf16[5120,512]{1,0:T(8,128)(2,1)} %bitcast.6, f32[1,5120]{1,0:T(1,128)} %bitcast.8, s32[4,32]{1,0:T(4,128)} %segments.1, s32[1,4]{1,0:T(1,128)} %bitcast.9, s32[4,32]{1,0:T(4,128)} %grades.1), custom_call_target="tpu_custom_call" | custom-call | tf_op jit(solution)/shard_map/pallas_call | solution.py:661
  163.2 1.9 %shard_map.87 = (f32[1,160,512]{2,1,0:T(8,128)}, f32[1,160,512]{2,1,0:T(8,128)}) custom-call(f32[160,512]{1,0:T(8,128)} %get-tuple-element.4.key_in, f32[160,512]{1,0:T(8,128)} %get-tuple-element.5.value_in), custom_call_target="tpu_custom_call" | custom-call | tf_op jit(solution)/shard_map/pallas_call | solution.py:726

commit v6 on v5

--- a/solution.py
+++ b/solution.py
@@ -14,7 +14,7 @@
 THETA = 1000000.0
 SUB = 16
 PIECES = 4
-BOUNDS = (0, 1024, 2048, 3072, 4096, 5120)
+BOUNDS = (0, 1024, 2048, 3072, 4096, 4608, 5120)
 STRIPS = len(BOUNDS) - 1
 MESH = pl.DeviceIdType.MESH
 F32 = jnp.float32
@@ -294,7 +294,7 @@
             device_id_type=MESH,
         )
 
-    def forward(c, n):
+    def forward(c, n, origin=False):
         some = pl.ds(c, n)
         lines = n * SUB
         row = c // 2
@@ -309,9 +309,9 @@
         for p in range(STRIPS):
             for k in range(n):
                 h_copy(c + k, p).wait_recv()
-            if n == 1:
-
-                @pl.when((section == 0) & (c == 0))
+            if origin:
+
+                @pl.when(c == 0)
                 def _():
                     for copy in load_weight(p):
                         copy.wait()
@@ -348,16 +348,8 @@
             if n == 1:
                 h_copy(c, p).start()
 
-        if n == 1:
-
-            @pl.when(section == 0)
-            def _():
-                ahead(lambda p: strip_of(p, dot_t(mixed, wv[columns(p), :])), send)
-
-            @pl.when(section > 0)
-            def _():
-                ahead(lambda p: strip_of(p, dot(mixed, wvt[:, columns(p)])), send)
-
+        if origin:
+            ahead(lambda p: strip_of(p, dot_t(mixed, wv[columns(p), :])), send)
         else:
             ahead(lambda p: strip_of(p, dot(mixed, wvt[:, columns(p)])), send)
 
@@ -392,7 +384,7 @@
             grad = first * wscore[:, columns(p)][None] - second * full
             gin[some, :, columns(p)] = grad.astype(BF16)
 
-    def backward(c, n):
+    def backward(c, n, origin=False):
         some = pl.ds(c, n)
         lines = n * SUB
         row = c // 2
@@ -432,28 +424,28 @@
         grad_key = turned * tall(cosine[some]) - swap(turned) * tall(sine[some])
         flat_key = unstack(grad_key.astype(BF16))
         flat_value = unstack(own_v.astype(BF16))
+        if not origin:
+
+            def strip_of(p):
+                grad = dot(flat_key, wkt[:, columns(p)]) + dot(flat_value, wvt[:, columns(p)])
+                full = hin[some, :, columns(p)].reshape(lines, -1).astype(F32)
+                out = grad_at(p).astype(F32) + scale * grad - along * full
+                return out.astype(BF16).reshape(n, SUB, -1)
+
+            def send(p, out):
+                gout[some, :, columns(p)] = out
+                g_copy(c + n - 1, p).start()
+
+            ahead(strip_of, send)
+            if n == 2:
+                for p in range(STRIPS):
+                    g_copy(c, p).start()
+
         features = HEADS * HD
         key_part = (flat_key.astype(F32) * scale).astype(BF16)
         value_part = (flat_value.astype(F32) * scale).astype(BF16)
         gkv[some, :, :features] = key_part.reshape(n, SUB, features)
         gkv[some, :, features:] = value_part.reshape(n, SUB, features)
-
-        @pl.when(section > 0)
-        def _():
-            def strip_of(p):
-                grad = dot(flat_key, wkt[:, columns(p)]) + dot(flat_value, wvt[:, columns(p)])
-                full = hin[some, :, columns(p)].reshape(lines, -1).astype(F32)
-                out = grad_at(p).astype(F32) + scale * grad - along * full
-                return out.astype(BF16).reshape(n, SUB, -1)
-
-            def send(p, out):
-                gout[some, :, columns(p)] = out
-                g_copy(c + n - 1, p).start()
-
-            ahead(strip_of, send)
-            if n == 2:
-                for p in range(STRIPS):
-                    g_copy(c, p).start()
 
         for k in range(n):
             for r in range(1, 4):
@@ -581,7 +573,11 @@
     lead = jnp.where(section == last - 1, 5, chunks)
 
     def slot(i, unused):
-        @pl.when(i < chunks)
+        @pl.when((i < chunks) & (section == 0))
+        def _():
+            forward(i, 1, True)
+
+        @pl.when((i < chunks) & (section > 0))
         def _():
             forward(i, 1)
 
@@ -591,9 +587,15 @@
         def _():
             turn(wk, wkt)
 
-        @pl.when((j >= 0) & (j < chunks))
+        c = (j // 2) * 2 + 1 - lax.rem(j, 2)
+
+        @pl.when((j >= 0) & (j < chunks) & (section == 0))
         def _():
-            backward((j // 2) * 2 + 1 - lax.rem(j, 2), 1)
+            backward(c, 1, True)
+
+        @pl.when((j >= 0) & (j < chunks) & (section > 0))
+        def _():
+            backward(c, 1)
 
         @pl.when((j == group + 1) & (section == 0))
         def _():

time: 165 us -> 163 us (0.988)
  Pallas kernels: 164 us -> 162 us
    pallas_call x1, Pallas kernels: 163 us -> 161 us  [shards(): pl.pallas_call(functools.partial(pipe_kernel, sections), out_shape=[jax.S...]
where the time goes in v6:
time: 163 us
  Pallas kernels  162 us (99%)
    pallas_call x1, Pallas kernels, shards(): pl.pallas_call(functools.partial(pipe_kernel, sections), out_shape=[jax.S...  161 us

profile of v6, /device:TPU:1, one launch (start us, length us, event | category | flops | bytes accessed | tf_op | source)
XLA Modules:
  0.0 163.1 jit_solution(15474400296667950589)
XLA Ops:
  0.6 160.5 %shard_map.86 = (f32[160,512]{1,0:T(8,128)}, f32[160,512]{1,0:T(8,128)}) custom-call(bf16[8,16,5120]{2,1,0:T(8,128)(2,1)} %bitcast.7, bf16[5120,512]{1,0:T(8,128)(2,1)} %bitcast.5, bf16[5120,512]{1,0:T(8,128)(2,1)} %bitcast.6, f32[1,5120]{1,0:T(1,128)} %bitcast.8, s32[4,32]{1,0:T(4,128)} %segments.1, s32[1,4]{1,0:T(1,128)} %bitcast.9, s32[4,32]{1,0:T(4,128)} %grades.1), custom_call_target="tpu_custom_call" | custom-call | tf_op jit(solution)/shard_map/pallas_call | solution.py:663
  161.1 1.9 %shard_map.87 = (f32[1,160,512]{2,1,0:T(8,128)}, f32[1,160,512]{2,1,0:T(8,128)}) custom-call(f32[160,512]{1,0:T(8,128)} %get-tuple-element.4.key_in, f32[160,512]{1,0:T(8,128)} %get-tuple-element.5.value_in), custom_call_target="tpu_custom_call" | custom-call | tf_op jit(solution)/shard_map/pallas_call | solution.py:728

commit v7 on v6

--- a/solution.py
+++ b/solution.py
@@ -354,7 +354,7 @@
             ahead(lambda p: strip_of(p, dot(mixed, wvt[:, columns(p)])), send)
 
         for k in range(n):
-            for r in range(1, 4):
+            for r in (2, 1, 3):
                 x_copy(0, c + k, r).start()
                 x_copy(1, c + k, r).start()
 
@@ -448,7 +448,7 @@
         gkv[some, :, features:] = value_part.reshape(n, SUB, features)
 
         for k in range(n):
-            for r in range(1, 4):
+            for r in (2, 1, 3):
                 x_copy(2, c + k, r).start()
                 x_copy(3, c + k, r).start()
 

time: 163 us -> 163 us (level)
  no operation moved by 1% of the time
where the time goes in v7:
time: 163 us
  Pallas kernels  162 us (99%)
    pallas_call x1, Pallas kernels, shards(): pl.pallas_call(functools.partial(pipe_kernel, sections), out_shape=[jax.S...  160 us

profile of v7, /device:TPU:1, one launch (start us, length us, event | category | flops | bytes accessed | tf_op | source)
XLA Modules:
  0.0 162.5 jit_solution(3993555561803653938)
XLA Ops:
  0.6 160.0 %shard_map.86 = (f32[160,512]{1,0:T(8,128)}, f32[160,512]{1,0:T(8,128)}) custom-call(bf16[8,16,5120]{2,1,0:T(8,128)(2,1)} %bitcast.7, bf16[5120,512]{1,0:T(8,128)(2,1)} %bitcast.5, bf16[5120,512]{1,0:T(8,128)(2,1)} %bitcast.6, f32[1,5120]{1,0:T(1,128)} %bitcast.8, s32[4,32]{1,0:T(4,128)} %segments.1, s32[1,4]{1,0:T(1,128)} %bitcast.9, s32[4,32]{1,0:T(4,128)} %grades.1), custom_call_target="tpu_custom_call" | custom-call | tf_op jit(solution)/shard_map/pallas_call | solution.py:663
  160.6 1.9 %shard_map.87 = (f32[1,160,512]{2,1,0:T(8,128)}, f32[1,160,512]{2,1,0:T(8,128)}) custom-call(f32[160,512]{1,0:T(8,128)} %get-tuple-element.4.key_in, f32[160,512]{1,0:T(8,128)} %get-tuple-element.5.value_in), custom_call_target="tpu_custom_call" | custom-call | tf_op jit(solution)/shard_map/pallas_call | solution.py:728
